TPU v7x, 32 devices: a whole 2x2x4 slice. The times are simulated.
32 devices in a mesh: dp: 4 (over y, x), head: 8 (over z, core).
Axes of the slice: x: 2, y: 2, z: 4, core: 2. Of those that a mesh axis runs over, the one named last changes fastest.
Arguments:
- query_latent: bfloat16 [1024, 1536], P('dp'), may hold values from -384 to 384
- kv_latent: bfloat16 [1024, 576], P('dp'), may hold values from -48 to 48
- out_grad: bfloat16 [1024, 4096], P('dp', 'head'), may hold values from -20 to 20
- query_up: bfloat16 [1536, 6144], P(None, 'head'), may hold values from -1 to 1
- key_up: bfloat16 [512, 4096], P(None, 'head'), may hold values from -0.25 to 0.25
- value_up: bfloat16 [512, 4096], P(None, 'head'), may hold values from -0.25 to 0.25
Outputs:
- query_latent_grad: float32 [1024, 1536], P(('dp', 'head'))
- kv_latent_grad: float32 [1024, 576], P(('dp', 'head'))
- query_up_grad: bfloat16 [1536, 6144], P(None, 'head')
- key_up_grad: bfloat16 [512, 4096], P(None, 'head')
- value_up_grad: bfloat16 [512, 4096], P(None, 'head')
All inputs are finite; a program needn't handle non-finite values.
Results may differ from a plain program's by a relative error of at most 0.035.
Values may be sent and summed in bfloat16 or wider, within the bound.
No kernel may reach another device: no remote copies, remote signals or barrier semaphores. Data moves between devices by JAX's collectives and lax.ppermute only.
A program may use at most 64 MiB of HBM per device.

v0:
```python
import functools

import jax
import jax.numpy as jnp
import numpy as np
from jax import lax
from jax.experimental import pallas as pl
from jax.experimental.pallas import tpu as pltpu
from jax.sharding import PartitionSpec as P

QL = 1536
KL = 512
DN = 128
DR = 64
TILE = 128
WIDTH = DN + DR
PAIR = 2 * WIDTH
LATENT = QL + KL + DR

max_rms = 1.0
eps = 1e-06
VMEM_LIMIT = 32 * 2**20

NT = (((1,), (1,)), ((), ()))
TN = (((0,), (0,)), ((), ()))


def dot(left, right, dims=(((1,), (0,)), ((), ()))):
    return lax.dot_general(left, right, dims, preferred_element_type=jnp.float32)


def rotary_tables(length):
    half = DR // 2
    freqs = np.float32(10000.0) ** (
        np.float32(-2.0) * np.arange(half, dtype=np.float32) / np.float32(DR)
    )
    angle = np.arange(length, dtype=np.float32)[:, None] * freqs.astype(np.float32)[None, :]
    cosine, sine = np.cos(angle), np.sin(angle)
    ones, zeros = np.ones((length, DR), np.float32), np.zeros((length, DR), np.float32)
    return np.concatenate([cosine, cosine, ones, -sine, sine, zeros], axis=1)


def swap_halves(tile):
    lane = lax.broadcasted_iota(jnp.int32, tile.shape, 1)
    first = lane % DR < DR // 2
    return jnp.where(
        first, pltpu.roll(tile, TILE - DR // 2, 1), pltpu.roll(tile, DR // 2, 1)
    )


def rounded(values):
    return values.astype(jnp.bfloat16).astype(jnp.float32)


def softmax_grads(scores, grad_probs):
    length = scores.shape[0]
    block = length // 2
    scale = 1.0 / (DN + DR) ** 0.5
    key = lax.broadcasted_iota(jnp.int32, (block, block), 0)
    query = lax.broadcasted_iota(jnp.int32, (block, block), 1)
    allowed = key <= query
    grad_probs = rounded(grad_probs)
    probs_columns, grads_columns = [], []
    for column in range(2):
        columns = slice(column * block, (column + 1) * block)
        parts = [scores[:block, columns], scores[block:, columns]][: column + 1]
        parts[-1] = jnp.where(allowed, parts[-1], -jnp.inf)
        tops = [jnp.max(part, axis=0, keepdims=True) for part in parts]
        top = tops[0] if column == 0 else jnp.maximum(*tops)
        parts = [jnp.exp((part - top) * scale) for part in parts]
        sums = [jnp.sum(part, axis=0, keepdims=True) for part in parts]
        inverse = 1.0 / (sums[0] if column == 0 else sums[0] + sums[1])
        parts = [part * inverse for part in parts]
        grads = [grad_probs[:block, columns], grad_probs[block:, columns]][: column + 1]
        means = [jnp.sum(g * p, axis=0, keepdims=True) for g, p in zip(grads, parts)]
        mean = means[0] if column == 0 else means[0] + means[1]
        grads = [(p * (g - mean) * scale).astype(jnp.bfloat16) for g, p in zip(grads, parts)]
        parts = [p.astype(jnp.bfloat16) for p in parts]
        if column == 0:
            parts.append(jnp.zeros((block, block), jnp.bfloat16))
            grads.append(jnp.zeros((block, block), jnp.bfloat16))
        probs_columns.append(jnp.concatenate(parts, axis=0))
        grads_columns.append(jnp.concatenate(grads, axis=0))
    return jnp.concatenate(probs_columns, axis=1), jnp.concatenate(grads_columns, axis=1)


def backward(length, xq, xkv, grad, weights, table, gq, gkv, qw, kw, vw, rot_out, ready):
    wq, wk, wv = weights
    n_seq = xq.shape[0] // length
    wide = wk.shape[1]
    heads = wide // DN
    low = lax.broadcasted_iota(jnp.int32, (length, TILE), 1) < DR
    spans = [slice(s * length, (s + 1) * length) for s in range(n_seq)]

    ready[0]()
    cos_low, sin_low = table[:, :TILE], table[:, TILE:]
    cos_tiles = (cos_low, pltpu.roll(cos_low, DR, 1))
    sin_tiles = (sin_low, pltpu.roll(sin_low, DR, 1))
    latent = xkv[:, :KL]
    for pair in range(heads // 2):
        columns = slice(2 * DN * pair, 2 * DN * (pair + 1))
        keys = dot(latent, wk[:, columns])
        vw[:, columns] = dot(latent, wv[:, columns]).astype(jnp.bfloat16)
        for span in spans:
            rot = jnp.concatenate(
                [xkv[span, KL : KL + DR].astype(jnp.float32), jnp.zeros((length, DR), jnp.float32)],
                axis=1,
            )
            odd = pltpu.roll(keys[span, DN:], DR, 1)
            tiles = (
                keys[span, :DN],
                rot,
                jnp.where(low, 0.0, odd),
                jnp.where(low, odd, pltpu.roll(rot, DR, 1)),
            )
            for i, tile in enumerate(tiles):
                start = (4 * pair + i) * TILE
                kw[span, start : start + TILE] = tile.astype(jnp.bfloat16)
    ready[1]()
    for pair in range(heads // 2):
        queries = dot(xq[...], wq[:, PAIR * pair : PAIR * (pair + 1)])
        for span in spans:
            for i in range(3):
                part = rounded(queries[span, i * TILE : (i + 1) * TILE])
                if i > 0:
                    part = part * cos_tiles[i - 1] + swap_halves(part) * sin_tiles[i - 1]
                start = PAIR * pair + i * TILE
                qw[span, start : start + TILE] = part.astype(jnp.bfloat16)

    items = [(span, head) for span in spans for head in range(heads)]

    def windows(span, head):
        start = PAIR * (head // 2) + TILE * (head % 2)
        return (
            qw[span, start : start + 2 * TILE],
            kw[span, 2 * TILE * head : 2 * TILE * (head + 1)],
            slice(head * DN, (head + 1) * DN),
        )

    def first_products(span, head):
        query_window, key_window, columns = windows(span, head)
        return (
            dot(key_window, query_window, NT),
            dot(vw[span, columns], grad[span, columns], NT),
        )

    rot_sums = [jnp.zeros((length, TILE), jnp.float32) for _ in spans]
    pending = first_products(*items[0])
    even_part = None
    for index, (span, head) in enumerate(items):
        products = pending
        if index + 1 < len(items):
            pending = first_products(*items[index + 1])
        probs, grad_scores = softmax_grads(*products)
        query_window, key_window, columns = windows(span, head)
        gkv[span, wide + head * DN : wide + (head + 1) * DN] = dot(probs, grad[span, columns]).astype(
            jnp.bfloat16
        )
        key_part = dot(grad_scores, query_window)
        query_part = dot(grad_scores, key_window, TN)
        seq = index // heads
        if head % 2 == 0:
            gkv[span, columns] = key_part[:, :TILE].astype(jnp.bfloat16)
            if rot_out is not None:
                rot_sums[seq] = rot_sums[seq] + rounded(key_part[:, TILE:])
            even_part = query_part
            continue
        turned = pltpu.roll(key_part[:, TILE:], DR, 1)
        gkv[span, columns] = jnp.where(low, pltpu.roll(key_part[:, :TILE], DR, 1), turned).astype(
            jnp.bfloat16
        )
        if rot_out is not None:
            rot_sums[seq] = rot_sums[seq] + rounded(turned)
        parts = [
            even_part[:, :TILE],
            even_part[:, TILE:] + query_part[:, :TILE],
            query_part[:, TILE:],
        ]
        for i in range(3):
            part = parts[i]
            if i > 0:
                part = rounded(part)
                part = part * cos_tiles[i - 1] - swap_halves(part) * sin_tiles[i - 1]
            start = PAIR * (head // 2) + i * TILE
            gq[span, start : start + TILE] = part.astype(jnp.bfloat16)
    if rot_out is not None:
        rot_out[...] = rot_sums[0]


def raw_grads(parts, left, right, sums, previous):
    wide = right.shape[1] // parts
    total = jnp.zeros((8, TILE), jnp.float32)
    for start in range(0, sums[0].shape[0], KL):
        rows = slice(start, start + KL)
        product = dot(left[:, rows], right[...], TN)
        for part in range(parts):
            block = product[:, part * wide : (part + 1) * wide]
            if previous is not None:
                block = block + previous[part][rows, :]
            sums[part][rows, :] = block
            folded = jnp.sum((block * block).reshape(KL // 8, 8, wide), axis=0)
            for column in range(0, wide, TILE):
                total = total + folded[:, column : column + TILE]
    return total


def load_kernel(place, xq, kvt, grad, packed, kv_rows, sem):
    half, wide = packed.shape[0], grad.shape[1]
    width = QL + KL + TILE
    rows = pl.ds(pl.multiple_of(place[1] * half, half), half)
    pieces = (
        (kvt.at[:, rows], kv_rows),
        (xq.at[rows], packed.at[:, :QL]),
        (grad.at[:half], packed.at[:, width : width + wide]),
        (grad.at[half:], packed.at[:, width + wide :]),
    )
    copies = [pltpu.make_async_copy(*piece, sem.at[i]) for i, piece in enumerate(pieces)]
    for copy in copies:
        copy.start()
    copies[0].wait()
    for block in range(0, KL + DR, TILE):
        stop = min(block + TILE, KL + DR)
        packed[:, QL + block : QL + stop] = kv_rows[block:stop, :].T
    packed[:, LATENT:width] = jnp.zeros((half, TILE - DR), jnp.bfloat16)
    for copy in copies[1:]:
        copy.wait()


def own_kernel(n_head, place, xq_in, kvt_in, grad_in, wq_in, wk_in, wv_in, table_in, *refs):
    wq, wk, wv, table, xq, xkv, gq, gkv, keep, send_stay, send_go, *refs = refs
    kvt, grad, qw, kw, vw, term, sem = refs
    pieces = (
        (kvt_in, kvt),
        (table_in, table),
        (wk_in, wk),
        (wv_in, wv),
        (xq_in, xq),
        (wq_in, wq),
        (grad_in, grad),
    )
    copies = [pltpu.make_async_copy(*piece, sem.at[i]) for i, piece in enumerate(pieces)]
    for copy in copies:
        copy.start()

    def latents_ready():
        for copy in copies[:4]:
            copy.wait()
        for block in range(0, KL + DR, TILE):
            stop = min(block + TILE, KL + DR)
            xkv[:, block:stop] = kvt[block:stop, :].T

    def queries_ready():
        for copy in copies[4:]:
            copy.wait()

    length = xq.shape[0]
    rot = term.at[:, QL + KL :]
    ready = (latents_ready, queries_ready)
    backward(length, xq, xkv, grad, (wq, wk, wv), table, gq, gkv, qw, kw, vw, rot, ready)
    wide = wk.shape[1]
    term[:, :QL] = dot(gq[...], wq[...], NT)
    term[:, QL : QL + KL] = dot(gkv[:, :wide], wk[...], NT) + dot(gkv[:, wide:], wv[...], NT)
    rows = length // n_head
    chip, core = place[0], place[1]
    masks = [turned_round(k, n_head // 2) for k in range(n_head // 2)]

    def chosen(which):
        starts = [(2 * jnp.bitwise_xor(chip, mask) + which) * rows for mask in masks]
        return jnp.concatenate([term[pl.ds(pl.multiple_of(i, rows), rows), :] for i in starts])

    keep[...] = chosen(core)
    send = chosen(1 - core).astype(jnp.bfloat16)
    send_stay[...] = send[: send_stay.shape[0], :]
    send_go[...] = send[send_stay.shape[0] :, :]


def fold_kernel(keep, *refs):
    received, (stay, go) = refs[:-2], refs[-2:]
    total = jnp.concatenate([part[...] for part in received]).astype(jnp.float32) + keep[...]
    stay[...] = total[: stay.shape[0], :]
    go[...] = total[stay.shape[0] :, :].astype(jnp.bfloat16)


def far_kernel(n_seq, place, *refs):
    blocks, refs = refs[: 2 * n_seq], refs[2 * n_seq :]
    wq, wk, wv, table, xq, xkv, gq, gkv, grad, qw, kw, vw = refs
    half, wide = blocks[0].shape[0], grad.shape[1]
    length = 2 * half
    width = QL + KL + TILE
    core = place[1]
    for s in range(n_seq):
        mine, other = blocks[2 * s : 2 * s + 2]
        for source, side in ((mine, core), (other, 1 - core)):
            rows = pl.ds(pl.multiple_of(s * length + side * half, half), half)
            xq[rows, :] = source[:, :QL]
            xkv[rows, :] = source[:, QL:LATENT]
        start = s * length
        grad[start : start + half, :] = mine[:, width : width + wide]
        grad[start + half : start + length, :] = mine[:, width + wide :]
    ready = (lambda: None, lambda: None)
    backward(length, xq, xkv, grad, (wq, wk, wv), table, gq, gkv, qw, kw, vw, None, ready)


def sums_kernel(parts, first, left, right, *refs):
    previous, sums = (None, refs) if first else (refs[:parts], refs[parts:])
    raw_grads(parts, left, right, sums, previous)


def last_kernel(xq, xkv, gq, gkv, pq, pk, pv, sq, sk, sv, squares):
    squares[...] = raw_grads(1, xq, gq, (sq,), (pq,)) + raw_grads(2, xkv, gkv, (sk, sv), (pk, pv))


def add_kernel(left, right, out):
    out[...] = left[...] + right[...]


def scale_kernel(limit, local, received, sq, sk, sv, *refs):
    *parts, oq, ok, ov, latent_q, latent_kv, bq, bk, bv, sem = refs
    total = parts[0][...]
    for part in parts[1:]:
        total = total + part[...]
    total = jnp.sum(total, keepdims=True)
    factor = jnp.minimum(1.0, limit / jnp.sqrt(total + eps))
    copies = []
    for source, buffer, out in ((sq, bq, oq), (sk, bk, ok), (sv, bv, ov)):
        for start in range(0, source.shape[0], 256):
            rows = slice(start, start + 256)
            buffer[rows, :] = (source[rows, :] * factor).astype(jnp.bfloat16)
            copy = pltpu.make_async_copy(buffer.at[rows], out.at[rows], sem.at[len(copies)])
            copy.start()
            copies.append(copy)
    terms = local[...] + received[...].astype(jnp.float32)
    latent_q[...] = terms[:, :QL]
    latent_kv[...] = terms[:, QL:LATENT]
    for copy in copies:
        copy.wait()


def vmem(count):
    return [pl.BlockSpec(memory_space=pltpu.VMEM)] * count


def hbm(count):
    return [pl.BlockSpec(memory_space=pltpu.HBM)] * count


def params():
    return pltpu.CompilerParams(vmem_limit_bytes=VMEM_LIMIT)


def free():
    return pl.CostEstimate(flops=0, bytes_accessed=0, transcendentals=0)


def struct(shape, dtype):
    return jax.ShapeDtypeStruct(shape, dtype)


def exchange(value, axis, size, k):
    return lax.ppermute(value, axis, [(i, i ^ k) for i in range(size)])


def far_away(value):
    return pltpu.with_memory_space_constraint(value, pltpu.HBM)


def turned_round(mask, n_dp):
    bits = n_dp.bit_length() - 1
    return sum(((mask >> i) & 1) << (bits - 1 - i) for i in range(bits))


def across(value, n_dp, n_head, mask):
    masks = (mask, turned_round(mask, n_dp))
    pairs = [
        (d * n_head + h, (d ^ masks[h % 2]) * n_head + h) for d in range(n_dp) for h in range(n_head)
    ]
    return lax.ppermute(value, ("dp", "head"), pairs)


def per_device(n_dp, n_head, query_latent, kv_latent, out_grad, query_up, key_up, value_up):
    length = query_latent.shape[0]
    half = length // 2
    wide_q, wide_k = query_up.shape[1], key_up.shape[1]
    heads = wide_k // DN
    index = lax.axis_index("head")
    place = jnp.stack([index // 2, index % 2]).astype(jnp.int32)
    table = jnp.asarray(rotary_tables(length))
    smem = [pl.BlockSpec(memory_space=pltpu.SMEM)]
    inputs = [far_away(value) for value in (query_latent, kv_latent.T, out_grad)]
    width = QL + KL + TILE

    packed = pl.pallas_call(
        load_kernel,
        out_shape=pltpu.VMEM((half, width + 2 * wide_k), jnp.bfloat16),
        in_specs=smem + hbm(3),
        out_specs=pl.BlockSpec(memory_space=pltpu.VMEM),
        scratch_shapes=[pltpu.VMEM((KL + DR, half), jnp.bfloat16), pltpu.SemaphoreType.DMA((4,))],
        compiler_params=params(),
        cost_estimate=free(),
        name="load",
    )(place, *inputs)
    packed, place = lax.optimization_barrier((packed, place))
    singles = [1 << i for i in reversed(range(n_dp.bit_length() - 1))]
    received = {k: across(packed, n_dp, n_head, k) for k in singles}

    def rows_shape(rows):
        widths = (QL, KL + DR, wide_q, 2 * wide_k)
        return tuple(pltpu.VMEM((rows, width), jnp.bfloat16) for width in widths)

    def scratch(rows):
        widths = (wide_k, wide_q, 2 * TILE * heads, wide_k)
        return [pltpu.VMEM((rows, width), jnp.bfloat16) for width in widths]

    weights_shape = tuple(
        pltpu.VMEM(shape, jnp.bfloat16) for shape in ((QL, wide_q), (KL, wide_k), (KL, wide_k))
    )
    sums_shape = tuple(pltpu.VMEM(w.shape, jnp.float32) for w in weights_shape)
    *outs, keep, send_stay, send_go = pl.pallas_call(
        functools.partial(own_kernel, n_head),
        out_shape=(
            *weights_shape,
            pltpu.VMEM(table.shape, jnp.float32),
            *rows_shape(length),
            struct((half, width), jnp.float32),
            struct((half // 2, width), jnp.bfloat16),
            struct((half // 2, width), jnp.bfloat16),
        ),
        in_specs=smem + hbm(7),
        out_specs=vmem(11),
        scratch_shapes=[pltpu.VMEM((KL + DR, length), jnp.bfloat16)]
        + scratch(length)
        + [pltpu.VMEM((length, width), jnp.float32), pltpu.SemaphoreType.DMA((7,))],
        compiler_params=params(),
        cost_estimate=free(),
        name="own",
    )(place, *inputs, *[far_away(value) for value in (query_up, key_up, value_up, table)])
    weights, found = outs[:4], outs[4:]

    rows = length // n_head
    squares_shape = struct((8, TILE), jnp.float32)

    def add_sums(left, right, shapes, sums):
        return list(
            pl.pallas_call(
                functools.partial(sums_kernel, len(shapes), not sums),
                out_shape=shapes,
                in_specs=vmem(2 + len(sums)),
                out_specs=vmem(len(shapes)),
                input_output_aliases={2 + i: i for i in range(len(sums))},
                compiler_params=params(),
                cost_estimate=free(),
                name="sums",
            )(left, right, *sums)
        )

    def add(left, right):
        return pl.pallas_call(
            add_kernel,
            out_shape=squares_shape,
            in_specs=vmem(2),
            out_specs=pl.BlockSpec(memory_space=pltpu.VMEM),
            compiler_params=params(),
            cost_estimate=free(),
            name="add",
        )(left, right)

    sums = add_sums(found[0], found[2], sums_shape[:1], [])
    sums += add_sums(found[1], found[3], sums_shape[1:], [])

    def fold(keep, *received):
        half_shape = (keep.shape[0] // 2, width)
        return pl.pallas_call(
            fold_kernel,
            out_shape=(struct(half_shape, jnp.float32), struct(half_shape, jnp.bfloat16)),
            in_specs=vmem(1 + len(received)),
            out_specs=vmem(2),
            compiler_params=params(),
            cost_estimate=free(),
            name="fold",
        )(keep, *received)

    stay, go = fold(keep, *[exchange(send, "head", n_head, 1) for send in (send_stay, send_go)])
    bits = [2 << i for i in range(n_head.bit_length() - 2)]
    for bit in bits[:-2]:
        stay, go = fold(stay, exchange(go, "head", n_head, bit))
    came = exchange(go, "head", n_head, bits[-2])

    values = [received[k] for k in singles]
    *values, sums[0], sums[2], came = lax.optimization_barrier((*values, sums[0], sums[2], came))
    received = dict(zip(singles, values))
    for k in range(3, n_dp):
        if k not in received:
            received[k] = across(received[k & (k - 1)], n_dp, n_head, k & -k)
    def swapped(k):
        return exchange(received[turned_round(k, n_dp)], "head", n_head, 1)

    groups = [(1, 2)] + [(k,) for k in range(3, n_dp)]
    for group in groups:
        n_seq = len(group)
        blocks = []
        for k in group:
            blocks += [received[k], swapped(k)]
        if group is not groups[0]:
            blocks[1], sums[1] = lax.optimization_barrier((blocks[1], sums[1]))
        found = list(
            pl.pallas_call(
                functools.partial(far_kernel, n_seq),
                out_shape=rows_shape(n_seq * length),
                in_specs=smem + vmem(len(blocks) + 4),
                out_specs=vmem(4),
                scratch_shapes=scratch(n_seq * length),
                compiler_params=params(),
                cost_estimate=free(),
                name="far",
            )(place, *blocks, *weights)
        )
        if group is groups[-1]:
            break
        if group is groups[0]:
            came, found[3] = lax.optimization_barrier((came, found[3]))
            stay, go = fold(stay, came)
            go, found[2] = lax.optimization_barrier((go, found[2]))
            terms = [stay, exchange(go, "head", n_head, bits[-1])]
        sums[:1] = add_sums(found[0], found[2], sums_shape[:1], sums[:1])
        k = groups[groups.index(group) + 1][0]
        received[k], sums[0] = lax.optimization_barrier((received[k], sums[0]))
        sums[1:] = add_sums(found[1], found[3], sums_shape[1:], sums[1:])

    *sums, squares = pl.pallas_call(
        last_kernel,
        out_shape=(*sums_shape, squares_shape),
        in_specs=vmem(4 + 3),
        out_specs=vmem(4),
        input_output_aliases={4: 0, 5: 1, 6: 2},
        compiler_params=params(),
        cost_estimate=free(),
        name="last",
    )(*found, *sums)

    count = (QL * wide_q + 2 * KL * wide_k) * n_head
    limit = max_rms * count**0.5
    squares = add(squares, exchange(squares, "head", n_head, 1))
    squares, terms[1] = lax.optimization_barrier((squares, terms[1]))
    parts = [squares] + [exchange(squares, "head", n_head, 2 * k) for k in range(1, n_head // 2)]
    *scaled, latent_q, latent_kv = pl.pallas_call(
        functools.partial(scale_kernel, limit),
        out_shape=(
            *[struct(w.shape, jnp.bfloat16) for w in weights_shape],
            struct((rows, QL), jnp.float32),
            struct((rows, KL + DR), jnp.float32),
        ),
        in_specs=vmem(2 + 3 + len(parts)),
        out_specs=hbm(3) + vmem(2),
        scratch_shapes=list(weights_shape)
        + [pltpu.SemaphoreType.DMA(((QL + 2 * KL) // 256,))],
        compiler_params=params(),
        cost_estimate=free(),
        name="scale",
    )(*terms, *sums, *parts)
    return (latent_q, latent_kv, *scaled)


def solution(mesh):
    placed = (
        P("dp", None),
        P("dp", None),
        P("dp", "head"),
        P(None, "head"),
        P(None, "head"),
        P(None, "head"),
    )
    return jax.shard_map(
        functools.partial(per_device, mesh.shape["dp"], mesh.shape["head"]),
        mesh=mesh,
        in_specs=placed,
        out_specs=(
            P(("dp", "head"), None),
            P(("dp", "head"), None),
            P(None, "head"),
            P(None, "head"),
            P(None, "head"),
        ),
        check_vma=False,
    )
```

profile of v0, /device:TPU:0, one launch (start us, length us, event | category | flops | bytes accessed | tf_op | source)
XLA Modules:
  0.0 60.2 jit_solution(7914879796549462717)
XLA Ops:
  0.7 1.7 %load.1 = bf16[128,3200]{1,0:T(8,128)(2,1)S(1)} custom-call(s32[2]{0:T(128)S(1)} %pad_add_fusion.place, bf16[256,1536]{1,0:T(8,128)(2,1)} %xq_in.1, bf16[576,256]{1,0:T(8,128)(2,1)} %bitcast.3, bf16[256,512]{1,0:T(8,128)(2,1)} %grad_in.1), custom_call_target="tpu_custom_call" | custom-call | tf_op jit(solution)/shard_map/load/pallas_call | solution.py:392
  2.5 3.0 %collective-permute-start.2 = (bf16[128,3200]{1,0:T(8,128)(2,1)S(1)}, bf16[128,3200]{1,0:T(8,128)(2,1)S(1)}, u32[]{:S(2)}, u32[]{:S(2)}) collective-permute-start(bf16[128,3200]{1,0:T(8,128)(2,1)S(1)} %load.1), channel_id=1, source_target_pairs={{0,16},{1,9},{2,18},{3,11},{4,20},{5,13},{6,22},{7,15},{8,24},{9,1... | collective-permute-start | bytes 2457608 | tf_op jit(solution)/shard_map/ppermute | solution.py:377
  5.5 1.5 %collective-permute-start.3 = (bf16[128,3200]{1,0:T(8,128)(2,1)S(1)}, bf16[128,3200]{1,0:T(8,128)(2,1)S(1)}, u32[]{:S(2)}, u32[]{:S(2)}) collective-permute-start(bf16[128,3200]{1,0:T(8,128)(2,1)S(1)} %load.1), channel_id=1, source_target_pairs={{0,8},{1,17},{2,10},{3,19},{4,12},{5,21},{6,14},{7,23},{8,0},{9,25... | collective-permute-start | bytes 2457608 | tf_op jit(solution)/shard_map/ppermute | solution.py:377
  7.0 6.1 %own.1 = (bf16[1536,768]{1,0:T(8,128)(2,1)S(1)}, bf16[512,512]{1,0:T(8,128)(2,1)S(1)}, bf16[512,512]{1,0:T(8,128)(2,1)S(1)}, f32[256,256]{1,0:T(8,128)S(1)}, bf1...) custom-call(s32[2]{0:T(128)S(1)} %pad_add_fusion.place, ...), custom_call_target="tpu_custom_call" | custom-call | tf_op jit(solution)/shard_map/own/pallas_call | solution.py:418
  13.2 0.5 collective-permute-start.1
  13.7 1.0 %collective-permute-done.refs_0_ = bf16[64,2176]{1,0:T(8,128)(2,1)S(1)} collective-permute-done((bf16[64,2176]{1,0:T(8,128)(2,1)S(1)}, bf16[64,2176]{1,0:T(8,128)(2,1)S(1)}, u32[]{:S(2)}, u32[]{:S(2)}) %collective-permute-start) | collective-permute-done | bytes 278560 | tf_op jit(solution)/shard_map/ppermute | solution.py:360
  15.3 1.6 %collective-permute-start.4 = (bf16[64,2176]{1,0:T(8,128)(2,1)S(1)}, bf16[64,2176]{1,0:T(8,128)(2,1)S(1)}, u32[]{:S(2)}, u32[]{:S(2)}) collective-permute-start(bf16[64,2176]{1,0:T(8,128)(2,1)S(1)} %get-tuple-element.69), channel_id=1, source_target_pairs={{0,2},{1,3},{2,0},{3,1},{4,6},{5,7},{6,4},{7,5},{8,10},{9,11},{10,... | collective-permute-start | bytes 835592 | tf_op jit(solution)/shard_map/ppermute | solution.py:360
  17.4 0.8 %sums.4.refs_0_ = f32[1536,768]{1,0:T(8,128)S(1)} custom-call(bf16[256,1536]{1,0:T(8,128)(2,1)S(1)} %get-tuple-element.64.left, bf16[256,768]{1,0:T(8,128)(2,1)S(1)} %get-tuple-element.65.right), custom_call_target="tpu_custom_call" | custom-call | tf_op jit(solution)/shard_map/sums/pallas_call | solution.py:444
  18.2 5.8 %collective-permute-done.4.refs_0_ = bf16[64,2176]{1,0:T(8,128)(2,1)S(1)} collective-permute-done((bf16[64,2176]{1,0:T(8,128)(2,1)S(1)}, bf16[64,2176]{1,0:T(8,128)(2,1)S(1)}, u32[]{:S(2)}, u32[]{:S(2)}) %collective-permute-start.4) | collective-permute-done | bytes 278560 | tf_op jit(solution)/shard_map/ppermute | solution.py:360
  24.6 1.5 %collective-permute-start.7 = (bf16[128,3200]{1,0:T(8,128)(2,1)S(1)}, bf16[128,3200]{1,0:T(8,128)(2,1)S(1)}, u32[]{:S(2)}, u32[]{:S(2)}) collective-permute-start(bf16[128,3200]{1,0:T(8,128)(2,1)S(1)} %collective-permute-done.2.refs_2_), channel_id=1, source_target_pairs={{0,8},{1,17},{2,10},{3,19},{4,12},{5,21},{6,14},{7,23},{8,0},{9,25... | collective-permute-start | bytes 2457608 | tf_op jit(solution)/shard_map/ppermute | solution.py:377
  26.4 1.2 %collective-permute-done.6.refs_3_ = bf16[128,3200]{1,0:T(8,128)(2,1)S(1)} collective-permute-done((bf16[128,3200]{1,0:T(8,128)(2,1)S(1)}, bf16[128,3200]{1,0:T(8,128)(2,1)S(1)}, u32[]{:S(2)}, u32[]{:S(2)}) %collective-permute-start.6) | collective-permute-done | bytes 819232 | tf_op jit(solution)/shard_map/ppermute | solution.py:360
  27.6 5.4 %far.2 = (bf16[512,1536]{1,0:T(8,128)(2,1)S(1)}, bf16[512,576]{1,0:T(8,128)(2,1)S(1)}, bf16[512,768]{1,0:T(8,128)(2,1)S(1)}, bf16[512,1024]{1,0:T(8,128)(2,1)S(1)}) custom-call(s32[2]{0:T(128)S(1)} %pad_add_fusion.place, bf16[128,3200]{1,0:T(8,128)(2,1)S(1)} %collective-permute-done.3.refs_0_, bf16[128,3200]{1,0:T(8,128)(2,1)S(1)} %collective-permute-done.5.refs_1_, ...), custom_call_target="tpu_custom_call" | custom-call | tf_op jit(solution)/shard_map/far/pallas_call | solution.py:506
  33.0 1.9 %sums.6.pq = f32[1536,768]{1,0:T(8,128)S(1)} custom-call(bf16[512,1536]{1,0:T(8,128)(2,1)S(1)} %get-tuple-element.80.left, bf16[512,768]{1,0:T(8,128)(2,1)S(1)} %get-tuple-element.83.right, f32[1536,768]{1,0:T(8,128)S(1)} %sums.4.refs_0_), custom_call_target="tpu_custom_call", output_to_operand_aliasing={{}: (2, {})} | custom-call | tf_op jit(solution)/shard_map/sums/pallas_call | solution.py:444
  34.9 2.0 %collective-permute-done.7.refs_0_ = bf16[128,3200]{1,0:T(8,128)(2,1)S(1)} collective-permute-done((bf16[128,3200]{1,0:T(8,128)(2,1)S(1)}, bf16[128,3200]{1,0:T(8,128)(2,1)S(1)}, u32[]{:S(2)}, u32[]{:S(2)}) %collective-permute-start.7) | collective-permute-done | bytes 819232 | tf_op jit(solution)/shard_map/ppermute | solution.py:377
  36.9 3.5 %collective-permute-start.10 = (bf16[32,2176]{1,0:T(8,128)(2,1)S(1)}, bf16[32,2176]{1,0:T(8,128)(2,1)S(1)}, u32[]{:S(2)}, u32[]{:S(2)}) collective-permute-start(bf16[32,2176]{1,0:T(8,128)(2,1)S(1)} %get-tuple-element.100), channel_id=1, source_target_pairs={{0,4},{1,5},{2,6},{3,7},{4,0},{5,1},{6,2},{7,3},{8,12},{9,13},{10,... | collective-permute-start | bytes 417800 | tf_op jit(solution)/shard_map/ppermute | solution.py:360
  40.5 0.8 %sums.7 = (f32[512,512]{1,0:T(8,128)S(1)}, f32[512,512]{1,0:T(8,128)S(1)}) custom-call(bf16[512,576]{1,0:T(8,128)(2,1)S(1)} %get-tuple-element.86.left, bf16[512,1024]{1,0:T(8,128)(2,1)S(1)} %get-tuple-element.87.right, f32[512,512]{1,0:T(8,128)S(1)} %get-tuple-element.88.refs_0_, ...), custom_call_target="tpu_custom_call", output_to_operand_aliasing={{0}: (2, {}), {1}: (3, {})} | custom-call | tf_op jit(solution)/shard_map/sums/pallas_call | solution.py:444
  41.3 3.3 %far.3 = (bf16[256,1536]{1,0:T(8,128)(2,1)S(1)}, bf16[256,576]{1,0:T(8,128)(2,1)S(1)}, bf16[256,768]{1,0:T(8,128)(2,1)S(1)}, bf16[256,1024]{1,0:T(8,128)(2,1)S(1)}) custom-call(s32[2]{0:T(128)S(1)} %pad_add_fusion.place, bf16[128,3200]{1,0:T(8,128)(2,1)S(1)} %collective-permute-done.7.refs_0_, bf16[128,3200]{1,0:T(8,128)(2,1)S(1)} %collective-permute-done.8.refs_1_, ...), custom_call_target="tpu_custom_call" | custom-call | tf_op jit(solution)/shard_map/far/pallas_call | solution.py:506
  44.6 2.0 %last.1 = (f32[1536,768]{1,0:T(8,128)S(1)}, f32[512,512]{1,0:T(8,128)S(1)}, f32[512,512]{1,0:T(8,128)S(1)}, f32[8,128]{1,0:T(8,128)S(1)}) custom-call(bf16[256,1536]{1,0:T(8,128)(2,1)S(1)} %get-tuple-element.92.xq, bf16[256,576]{1,0:T(8,128)(2,1)S(1)} %get-tuple-element.93.xkv, ...), custom_call_target="tpu_custom_call", output_to_operand_aliasing={{0}: (4, {}), {1}: (5, {}), {2}: (6, {})} | custom-call | tf_op jit(solution)/shard_map/last/pallas_call | solution.py:529
  46.9 0.9 %collective-permute-done.9.right = f32[8,128]{1,0:T(8,128)S(1)} collective-permute-done((f32[8,128]{1,0:T(8,128)S(1)}, f32[8,128]{1,0:T(8,128)S(1)}, u32[]{:S(2)}, u32[]{:S(2)}) %collective-permute-start.9) | collective-permute-done | bytes 4128 | tf_op jit(solution)/shard_map/ppermute | solution.py:360
  47.9 1.6 %collective-permute-start.11 = (f32[8,128]{1,0:T(8,128)S(1)}, f32[8,128]{1,0:T(8,128)S(1)}, u32[]{:S(2)}, u32[]{:S(2)}) collective-permute-start(f32[8,128]{1,0:T(8,128)S(1)} %add.9.refs_0_), channel_id=1, source_target_pairs={{0,2},{1,3},{2,0},{3,1},{4,6},{5,7},{6,4},{7,5},{8,10},{9,11},{10,... | collective-permute-start | bytes 12296 | tf_op jit(solution)/shard_map/ppermute | solution.py:360
  49.5 2.4 %collective-permute-start.12 = (f32[8,128]{1,0:T(8,128)S(1)}, f32[8,128]{1,0:T(8,128)S(1)}, u32[]{:S(2)}, u32[]{:S(2)}) collective-permute-start(f32[8,128]{1,0:T(8,128)S(1)} %add.9.refs_0_), channel_id=1, source_target_pairs={{0,4},{1,5},{2,6},{3,7},{4,0},{5,1},{6,2},{7,3},{8,12},{9,13},{10,... | collective-permute-start | bytes 12296 | tf_op jit(solution)/shard_map/ppermute | solution.py:360
  52.3 1.7 %collective-permute-done.12.refs_2_ = f32[8,128]{1,0:T(8,128)S(1)} collective-permute-done((f32[8,128]{1,0:T(8,128)S(1)}, f32[8,128]{1,0:T(8,128)S(1)}, u32[]{:S(2)}, u32[]{:S(2)}) %collective-permute-start.12) | collective-permute-done | bytes 4128 | tf_op jit(solution)/shard_map/ppermute | solution.py:360
  54.0 3.3 %collective-permute-done.13.refs_3_ = f32[8,128]{1,0:T(8,128)S(1)} collective-permute-done((f32[8,128]{1,0:T(8,128)S(1)}, f32[8,128]{1,0:T(8,128)S(1)}, u32[]{:S(2)}, u32[]{:S(2)}) %collective-permute-start.13) | collective-permute-done | bytes 4128 | tf_op jit(solution)/shard_map/ppermute | solution.py:360
  57.3 2.7 %scale.1 = (bf16[1536,768]{1,0:T(8,128)(2,1)}, bf16[512,512]{1,0:T(8,128)(2,1)}, bf16[512,512]{1,0:T(8,128)(2,1)}, f32[32,1536]{1,0:T(8,128)}, f32[32,576]{1,0:T(8,128)}) custom-call(f32[32,2176]{1,0:T(8,128)S(1)} %get-tuple-element.79.local, bf16[32,2176]{1,0:T(8,128)(2,1)S(1)} %collective-permute-done.10.received, f32[1536,768]{1,0:T(8,128)S(1)} %get-tuple-element.102.sq, ...), custom_call_target="tpu_custom_call" | custom-call | tf_op jit(solution)/shard_map/scale/pallas_call | solution.py:545
  (18 shorter events, 2.8 us)
Async XLA Ops:
  2.5 21.6 %collective-permute-start.2 = (bf16[128,3200]{1,0:T(8,128)(2,1)S(1)}, bf16[128,3200]{1,0:T(8,128)(2,1)S(1)}, u32[]{:S(2)}, u32[]{:S(2)}) collective-permute-start(bf16[128,3200]{1,0:T(8,128)(2,1)S(1)} %load.1), channel_id=1, source_target_pairs={{0,16},{1,9},{2,18},{3,11},{4,20},{5,13},{6,22},{7,15},{8,24},{9,1... | collective-permute-start | bytes 2457608 | tf_op jit(solution)/shard_map/ppermute | solution.py:377
  5.5 18.6 %collective-permute-start.3 = (bf16[128,3200]{1,0:T(8,128)(2,1)S(1)}, bf16[128,3200]{1,0:T(8,128)(2,1)S(1)}, u32[]{:S(2)}, u32[]{:S(2)}) collective-permute-start(bf16[128,3200]{1,0:T(8,128)(2,1)S(1)} %load.1), channel_id=1, source_target_pairs={{0,8},{1,17},{2,10},{3,19},{4,12},{5,21},{6,14},{7,23},{8,0},{9,25... | collective-permute-start | bytes 2457608 | tf_op jit(solution)/shard_map/ppermute | solution.py:377
  13.1 1.6 %collective-permute-start = (bf16[64,2176]{1,0:T(8,128)(2,1)S(1)}, bf16[64,2176]{1,0:T(8,128)(2,1)S(1)}, u32[]{:S(2)}, u32[]{:S(2)}) collective-permute-start(bf16[64,2176]{1,0:T(8,128)(2,1)S(1)} %get-tuple-element.60), channel_id=1, source_target_pairs={{0,1},{1,0},{2,3},{3,2},{4,5},{5,4},{6,7},{7,6},{8,9},{9,8},{10,11... | collective-permute-start | bytes 835592 | tf_op jit(solution)/shard_map/ppermute | solution.py:360
  13.2 1.9 %collective-permute-start.1 = (bf16[64,2176]{1,0:T(8,128)(2,1)S(1)}, bf16[64,2176]{1,0:T(8,128)(2,1)S(1)}, u32[]{:S(2)}, u32[]{:S(2)}) collective-permute-start(bf16[64,2176]{1,0:T(8,128)(2,1)S(1)} %get-tuple-element.61), channel_id=1, source_target_pairs={{0,1},{1,0},{2,3},{3,2},{4,5},{5,4},{6,7},{7,6},{8,9},{9,8},{10,11... | collective-permute-start | bytes 835592 | tf_op jit(solution)/shard_map/ppermute | solution.py:360
  15.3 8.8 %collective-permute-start.4 = (bf16[64,2176]{1,0:T(8,128)(2,1)S(1)}, bf16[64,2176]{1,0:T(8,128)(2,1)S(1)}, u32[]{:S(2)}, u32[]{:S(2)}) collective-permute-start(bf16[64,2176]{1,0:T(8,128)(2,1)S(1)} %get-tuple-element.69), channel_id=1, source_target_pairs={{0,2},{1,3},{2,0},{3,1},{4,6},{5,7},{6,4},{7,5},{8,10},{9,11},{10,... | collective-permute-start | bytes 835592 | tf_op jit(solution)/shard_map/ppermute | solution.py:360
  24.1 2.3 %collective-permute-start.5 = (bf16[128,3200]{1,0:T(8,128)(2,1)S(1)}, bf16[128,3200]{1,0:T(8,128)(2,1)S(1)}, u32[]{:S(2)}, u32[]{:S(2)}) collective-permute-start(bf16[128,3200]{1,0:T(8,128)(2,1)S(1)} %collective-permute-done.2.refs_2_), channel_id=1, source_target_pairs={{0,1},{1,0},{2,3},{3,2},{4,5},{5,4},{6,7},{7,6},{8,9},{9,8},{10,11... | collective-permute-start | bytes 2457608 | tf_op jit(solution)/shard_map/ppermute | solution.py:360
  24.4 3.2 %collective-permute-start.6 = (bf16[128,3200]{1,0:T(8,128)(2,1)S(1)}, bf16[128,3200]{1,0:T(8,128)(2,1)S(1)}, u32[]{:S(2)}, u32[]{:S(2)}) collective-permute-start(bf16[128,3200]{1,0:T(8,128)(2,1)S(1)} %collective-permute-done.3.refs_0_), channel_id=1, source_target_pairs={{0,1},{1,0},{2,3},{3,2},{4,5},{5,4},{6,7},{7,6},{8,9},{9,8},{10,11... | collective-permute-start | bytes 2457608 | tf_op jit(solution)/shard_map/ppermute | solution.py:360
  24.6 12.3 %collective-permute-start.7 = (bf16[128,3200]{1,0:T(8,128)(2,1)S(1)}, bf16[128,3200]{1,0:T(8,128)(2,1)S(1)}, u32[]{:S(2)}, u32[]{:S(2)}) collective-permute-start(bf16[128,3200]{1,0:T(8,128)(2,1)S(1)} %collective-permute-done.2.refs_2_), channel_id=1, source_target_pairs={{0,8},{1,17},{2,10},{3,19},{4,12},{5,21},{6,14},{7,23},{8,0},{9,25... | collective-permute-start | bytes 2457608 | tf_op jit(solution)/shard_map/ppermute | solution.py:377
  36.9 4.3 %collective-permute-start.8 = (bf16[128,3200]{1,0:T(8,128)(2,1)S(1)}, bf16[128,3200]{1,0:T(8,128)(2,1)S(1)}, u32[]{:S(2)}, u32[]{:S(2)}) collective-permute-start(bf16[128,3200]{1,0:T(8,128)(2,1)S(1)} %collective-permute-done.7.refs_0_), channel_id=1, source_target_pairs={{0,1},{1,0},{2,3},{3,2},{4,5},{5,4},{6,7},{7,6},{8,9},{9,8},{10,11... | collective-permute-start | bytes 2457608 | tf_op jit(solution)/shard_map/ppermute | solution.py:360
  36.9 11.0 %collective-permute-start.10 = (bf16[32,2176]{1,0:T(8,128)(2,1)S(1)}, bf16[32,2176]{1,0:T(8,128)(2,1)S(1)}, u32[]{:S(2)}, u32[]{:S(2)}) collective-permute-start(bf16[32,2176]{1,0:T(8,128)(2,1)S(1)} %get-tuple-element.100), channel_id=1, source_target_pairs={{0,4},{1,5},{2,6},{3,7},{4,0},{5,1},{6,2},{7,3},{8,12},{9,13},{10,... | collective-permute-start | bytes 417800 | tf_op jit(solution)/shard_map/ppermute | solution.py:360
  46.6 1.2 %collective-permute-start.9 = (f32[8,128]{1,0:T(8,128)S(1)}, f32[8,128]{1,0:T(8,128)S(1)}, u32[]{:S(2)}, u32[]{:S(2)}) collective-permute-start(f32[8,128]{1,0:T(8,128)S(1)} %get-tuple-element.99.left), channel_id=1, source_target_pairs={{0,1},{1,0},{2,3},{3,2},{4,5},{5,4},{6,7},{7,6},{8,9},{9,8},{10,11... | collective-permute-start | bytes 12296 | tf_op jit(solution)/shard_map/ppermute | solution.py:360
  47.9 4.4 %collective-permute-start.11 = (f32[8,128]{1,0:T(8,128)S(1)}, f32[8,128]{1,0:T(8,128)S(1)}, u32[]{:S(2)}, u32[]{:S(2)}) collective-permute-start(f32[8,128]{1,0:T(8,128)S(1)} %add.9.refs_0_), channel_id=1, source_target_pairs={{0,2},{1,3},{2,0},{3,1},{4,6},{5,7},{6,4},{7,5},{8,10},{9,11},{10,... | collective-permute-start | bytes 12296 | tf_op jit(solution)/shard_map/ppermute | solution.py:360
  49.5 4.5 %collective-permute-start.12 = (f32[8,128]{1,0:T(8,128)S(1)}, f32[8,128]{1,0:T(8,128)S(1)}, u32[]{:S(2)}, u32[]{:S(2)}) collective-permute-start(f32[8,128]{1,0:T(8,128)S(1)} %add.9.refs_0_), channel_id=1, source_target_pairs={{0,4},{1,5},{2,6},{3,7},{4,0},{5,1},{6,2},{7,3},{8,12},{9,13},{10,... | collective-permute-start | bytes 12296 | tf_op jit(solution)/shard_map/ppermute | solution.py:360
  51.9 5.4 %collective-permute-start.13 = (f32[8,128]{1,0:T(8,128)S(1)}, f32[8,128]{1,0:T(8,128)S(1)}, u32[]{:S(2)}, u32[]{:S(2)}) collective-permute-start(f32[8,128]{1,0:T(8,128)S(1)} %add.9.refs_0_), channel_id=1, source_target_pairs={{0,6},{1,7},{2,4},{3,5},{4,2},{5,3},{6,0},{7,1},{8,14},{9,15},{10,... | collective-permute-start | bytes 12296 | tf_op jit(solution)/shard_map/ppermute | solution.py:360
where the time goes:
time: 60.3 us; the launch traced here: 60.2 us
  Pallas kernels  25.5 us (42%)
  starting transfers between devices  16.9 us (28%)
  waiting for transfers between devices  16.8 us (28%)
  between operations  0.91 us (2%)
    ppermute x11, waiting for transfers between devices, exchange(): return lax.ppermute(value, axis, [(i, i ^ k) for i in range(size)])  14.8 us
    ppermute x11, starting transfers between devices, exchange(): return lax.ppermute(value, axis, [(i, i ^ k) for i in range(size)])  10.9 us
    pallas_call x2, Pallas kernels, per_device(): pl.pallas_call(functools.partial(far_kernel, n_seq), out_shape=rows_shape...  8.67 us
    pallas_call x1, Pallas kernels, per_device(): pl.pallas_call(functools.partial(own_kernel, n_head), out_shape=(*weights...  6.13 us
    ppermute x3, starting transfers between devices, across(): return lax.ppermute(value, ('dp', 'head'), pairs)  5.98 us
    pallas_call x4, Pallas kernels, add_sums(): pl.pallas_call(functools.partial(sums_kernel, len(shapes), not sums), out...  4.01 us
    pallas_call x1, Pallas kernels, per_device(): pl.pallas_call(functools.partial(scale_kernel, limit), out_shape=(*[struc...  2.73 us
    pallas_call x1, Pallas kernels, per_device(): pl.pallas_call(last_kernel, out_shape=(*sums_shape, squares_shape), in_sp...  2.04 us
  transfers between devices with their start and end apart: 14, of which 9 were waited for; matrix products, arithmetic and copies ran while one was open for 0% of the time, Pallas kernels for 35%

commit v1 on v0

--- a/solution.py
+++ b/solution.py
@@ -204,16 +204,10 @@
     return total
 
 
-def load_kernel(place, xq, kvt, grad, packed, kv_rows, sem):
-    half, wide = packed.shape[0], grad.shape[1]
-    width = QL + KL + TILE
+def load_kernel(place, xq, kvt, grad, packed, cotangent, kv_rows, sem):
+    half = packed.shape[0]
     rows = pl.ds(pl.multiple_of(place[1] * half, half), half)
-    pieces = (
-        (kvt.at[:, rows], kv_rows),
-        (xq.at[rows], packed.at[:, :QL]),
-        (grad.at[:half], packed.at[:, width : width + wide]),
-        (grad.at[half:], packed.at[:, width + wide :]),
-    )
+    pieces = ((kvt.at[:, rows], kv_rows), (xq.at[rows], packed.at[:, :QL]), (grad, cotangent))
     copies = [pltpu.make_async_copy(*piece, sem.at[i]) for i, piece in enumerate(pieces)]
     for copy in copies:
         copy.start()
@@ -221,13 +215,13 @@
     for block in range(0, KL + DR, TILE):
         stop = min(block + TILE, KL + DR)
         packed[:, QL + block : QL + stop] = kv_rows[block:stop, :].T
-    packed[:, LATENT:width] = jnp.zeros((half, TILE - DR), jnp.bfloat16)
+    packed[:, LATENT:] = jnp.zeros((half, TILE - DR), jnp.bfloat16)
     for copy in copies[1:]:
         copy.wait()
 
 
 def own_kernel(n_head, place, xq_in, kvt_in, grad_in, wq_in, wk_in, wv_in, table_in, *refs):
-    wq, wk, wv, table, xq, xkv, gq, gkv, keep, send_stay, send_go, *refs = refs
+    wq, wk, wv, table, xq, xkv, gq, gkv, keep, send, *refs = refs
     kvt, grad, qw, kw, vw, term, sem = refs
     pieces = (
         (kvt_in, kvt),
@@ -269,34 +263,28 @@
         return jnp.concatenate([term[pl.ds(pl.multiple_of(i, rows), rows), :] for i in starts])
 
     keep[...] = chosen(core)
-    send = chosen(1 - core).astype(jnp.bfloat16)
-    send_stay[...] = send[: send_stay.shape[0], :]
-    send_go[...] = send[send_stay.shape[0] :, :]
-
-
-def fold_kernel(keep, *refs):
-    received, (stay, go) = refs[:-2], refs[-2:]
-    total = jnp.concatenate([part[...] for part in received]).astype(jnp.float32) + keep[...]
+    send[...] = chosen(1 - core).astype(jnp.bfloat16)
+
+
+def fold_kernel(keep, received, stay, go):
+    total = keep[...] + received[...].astype(jnp.float32)
     stay[...] = total[: stay.shape[0], :]
     go[...] = total[stay.shape[0] :, :].astype(jnp.bfloat16)
 
 
 def far_kernel(n_seq, place, *refs):
-    blocks, refs = refs[: 2 * n_seq], refs[2 * n_seq :]
+    blocks, refs = refs[: 3 * n_seq], refs[3 * n_seq :]
     wq, wk, wv, table, xq, xkv, gq, gkv, grad, qw, kw, vw = refs
-    half, wide = blocks[0].shape[0], grad.shape[1]
+    half = blocks[0].shape[0]
     length = 2 * half
-    width = QL + KL + TILE
     core = place[1]
     for s in range(n_seq):
-        mine, other = blocks[2 * s : 2 * s + 2]
+        mine, other, cotangent = blocks[3 * s : 3 * s + 3]
         for source, side in ((mine, core), (other, 1 - core)):
             rows = pl.ds(pl.multiple_of(s * length + side * half, half), half)
             xq[rows, :] = source[:, :QL]
             xkv[rows, :] = source[:, QL:LATENT]
-        start = s * length
-        grad[start : start + half, :] = mine[:, width : width + wide]
-        grad[start + half : start + length, :] = mine[:, width + wide :]
+        grad[s * length : (s + 1) * length, :] = cotangent[...]
     ready = (lambda: None, lambda: None)
     backward(length, xq, xkv, grad, (wq, wk, wv), table, gq, gkv, qw, kw, vw, None, ready)
 
@@ -389,18 +377,22 @@
     inputs = [far_away(value) for value in (query_latent, kv_latent.T, out_grad)]
     width = QL + KL + TILE
 
-    packed = pl.pallas_call(
+    packed, cotangent = pl.pallas_call(
         load_kernel,
-        out_shape=pltpu.VMEM((half, width + 2 * wide_k), jnp.bfloat16),
+        out_shape=(
+            pltpu.VMEM((half, width), jnp.bfloat16),
+            pltpu.VMEM((length, wide_k), jnp.bfloat16),
+        ),
         in_specs=smem + hbm(3),
-        out_specs=pl.BlockSpec(memory_space=pltpu.VMEM),
-        scratch_shapes=[pltpu.VMEM((KL + DR, half), jnp.bfloat16), pltpu.SemaphoreType.DMA((4,))],
+        out_specs=vmem(2),
+        scratch_shapes=[pltpu.VMEM((KL + DR, half), jnp.bfloat16), pltpu.SemaphoreType.DMA((3,))],
         compiler_params=params(),
         cost_estimate=free(),
         name="load",
     )(place, *inputs)
     packed, place = lax.optimization_barrier((packed, place))
     singles = [1 << i for i in reversed(range(n_dp.bit_length() - 1))]
+    cotangents = {k: across(cotangent, n_dp, n_head, k) for k in singles}
     received = {k: across(packed, n_dp, n_head, k) for k in singles}
 
     def rows_shape(rows):
@@ -415,18 +407,17 @@
         pltpu.VMEM(shape, jnp.bfloat16) for shape in ((QL, wide_q), (KL, wide_k), (KL, wide_k))
     )
     sums_shape = tuple(pltpu.VMEM(w.shape, jnp.float32) for w in weights_shape)
-    *outs, keep, send_stay, send_go = pl.pallas_call(
+    *outs, keep, send = pl.pallas_call(
         functools.partial(own_kernel, n_head),
         out_shape=(
             *weights_shape,
             pltpu.VMEM(table.shape, jnp.float32),
             *rows_shape(length),
             struct((half, width), jnp.float32),
-            struct((half // 2, width), jnp.bfloat16),
-            struct((half // 2, width), jnp.bfloat16),
+            struct((half, width), jnp.bfloat16),
         ),
         in_specs=smem + hbm(7),
-        out_specs=vmem(11),
+        out_specs=vmem(10),
         scratch_shapes=[pltpu.VMEM((KL + DR, length), jnp.bfloat16)]
         + scratch(length)
         + [pltpu.VMEM((length, width), jnp.float32), pltpu.SemaphoreType.DMA((7,))],
@@ -467,30 +458,36 @@
     sums = add_sums(found[0], found[2], sums_shape[:1], [])
     sums += add_sums(found[1], found[3], sums_shape[1:], [])
 
-    def fold(keep, *received):
+    def fold(keep, received):
         half_shape = (keep.shape[0] // 2, width)
         return pl.pallas_call(
             fold_kernel,
             out_shape=(struct(half_shape, jnp.float32), struct(half_shape, jnp.bfloat16)),
-            in_specs=vmem(1 + len(received)),
+            in_specs=vmem(2),
             out_specs=vmem(2),
             compiler_params=params(),
             cost_estimate=free(),
             name="fold",
-        )(keep, *received)
-
-    stay, go = fold(keep, *[exchange(send, "head", n_head, 1) for send in (send_stay, send_go)])
+        )(keep, received)
+
+    stay, go = fold(keep, exchange(send, "head", n_head, 1))
     bits = [2 << i for i in range(n_head.bit_length() - 2)]
     for bit in bits[:-2]:
         stay, go = fold(stay, exchange(go, "head", n_head, bit))
     came = exchange(go, "head", n_head, bits[-2])
 
     values = [received[k] for k in singles]
-    *values, sums[0], sums[2], came = lax.optimization_barrier((*values, sums[0], sums[2], came))
+    *values, sums[0], sums[2] = lax.optimization_barrier((*values, sums[0], sums[2]))
     received = dict(zip(singles, values))
+    values = [cotangents[k] for k in singles]
+    relayed, *values = lax.optimization_barrier((received, *values))
+    cotangents = dict(zip(singles, values))
     for k in range(3, n_dp):
         if k not in received:
-            received[k] = across(received[k & (k - 1)], n_dp, n_head, k & -k)
+            relayed[k] = across(relayed[k & (k - 1)], n_dp, n_head, k & -k)
+            received[k] = relayed[k]
+            cotangents[k] = across(cotangents[k & (k - 1)], n_dp, n_head, k & -k)
+
     def swapped(k):
         return exchange(received[turned_round(k, n_dp)], "head", n_head, 1)
 
@@ -499,7 +496,7 @@
         n_seq = len(group)
         blocks = []
         for k in group:
-            blocks += [received[k], swapped(k)]
+            blocks += [received[k], swapped(k), cotangents[k]]
         if group is not groups[0]:
             blocks[1], sums[1] = lax.optimization_barrier((blocks[1], sums[1]))
         found = list(
@@ -516,14 +513,19 @@
         )
         if group is groups[-1]:
             break
+        k = groups[groups.index(group) + 1][0]
         if group is groups[0]:
             came, found[3] = lax.optimization_barrier((came, found[3]))
             stay, go = fold(stay, came)
-            go, found[2] = lax.optimization_barrier((go, found[2]))
+            received[k], go, found[2], found[3] = lax.optimization_barrier(
+                (received[k], go, found[2], found[3])
+            )
             terms = [stay, exchange(go, "head", n_head, bits[-1])]
+        else:
+            received[k], found[2], found[3] = lax.optimization_barrier(
+                (received[k], found[2], found[3])
+            )
         sums[:1] = add_sums(found[0], found[2], sums_shape[:1], sums[:1])
-        k = groups[groups.index(group) + 1][0]
-        received[k], sums[0] = lax.optimization_barrier((received[k], sums[0]))
         sums[1:] = add_sums(found[1], found[3], sums_shape[1:], sums[1:])
 
     *sums, squares = pl.pallas_call(

time: 60.3 us -> 60.9 us (level)
  waiting for transfers between devices: 16.8 us -> 18 us
    ppermute x3 -> x6, waiting for transfers between devices: 2.02 us -> 9.34 us  [across(): return lax.ppermute(value, ('dp', 'head'), pairs)]
    ppermute x11 -> x10, waiting for transfers between devices: 14.8 us -> 8.65 us  [exchange(): return lax.ppermute(value, axis, [(i, i ^ k) for i in range(size)])]
    ppermute x11 -> x10, starting transfers between devices: 10.9 us -> 9.58 us  [exchange(): return lax.ppermute(value, axis, [(i, i ^ k) for i in range(size)])]
    ppermute x3 -> x6, starting transfers between devices: 5.98 us -> 6.73 us  [across(): return lax.ppermute(value, ('dp', 'head'), pairs)]
  transfers between devices with their start and end apart: 14 -> 16, of which waited for: 9 -> 8; matrix products, arithmetic and copies ran while one was open for 0% -> 0% of each run, Pallas kernels for 35% -> 35%
where the time goes in v1:
time: 60.9 us; the launch traced here: 60.7 us
  Pallas kernels  25.4 us (42%)
  waiting for transfers between devices  18 us (30%)
  starting transfers between devices  16.3 us (27%)
  between operations  0.93 us (2%)
    ppermute x10, starting transfers between devices, exchange(): return lax.ppermute(value, axis, [(i, i ^ k) for i in range(size)])  9.58 us
    ppermute x6, waiting for transfers between devices, across(): return lax.ppermute(value, ('dp', 'head'), pairs)  9.34 us
    ppermute x10, waiting for transfers between devices, exchange(): return lax.ppermute(value, axis, [(i, i ^ k) for i in range(size)])  8.65 us
    pallas_call x2, Pallas kernels, per_device(): pl.pallas_call(functools.partial(far_kernel, n_seq), out_shape=rows_shape...  8.6 us
    ppermute x6, starting transfers between devices, across(): return lax.ppermute(value, ('dp', 'head'), pairs)  6.73 us
    pallas_call x1, Pallas kernels, per_device(): pl.pallas_call(functools.partial(own_kernel, n_head), out_shape=(*weights...  6.13 us
    pallas_call x4, Pallas kernels, add_sums(): pl.pallas_call(functools.partial(sums_kernel, len(shapes), not sums), out...  4.02 us
    pallas_call x1, Pallas kernels, per_device(): pl.pallas_call(functools.partial(scale_kernel, limit), out_shape=(*[struc...  2.73 us
  transfers between devices with their start and end apart: 16, of which 8 were waited for; matrix products, arithmetic and copies ran while one was open for 0% of the time, Pallas kernels for 35%

profile of v1, /device:TPU:0, one launch (start us, length us, event | category | flops | bytes accessed | tf_op | source)
XLA Modules:
  0.0 60.7 jit_solution(5377767860994751062)
XLA Ops:
  0.7 1.7 %load.1 = (bf16[128,2176]{1,0:T(8,128)(2,1)S(1)}, bf16[256,512]{1,0:T(8,128)(2,1)S(1)}) custom-call(s32[2]{0:T(128)S(1)} %pad_add_fusion.place, bf16[256,1536]{1,0:T(8,128)(2,1)} %xq_in.1, bf16[576,256]{1,0:T(8,128)(2,1)} %bitcast.3, bf16[256,512]{1,0:T(8,128)(2,1)} %grad_in.1), custom_call_target="tpu_custom_call" | custom-call | tf_op jit(solution)/shard_map/load/pallas_call | solution.py:380
  2.4 3.0 %collective-permute-start.2 = (bf16[128,2176]{1,0:T(8,128)(2,1)S(1)}, bf16[128,2176]{1,0:T(8,128)(2,1)S(1)}, u32[]{:S(2)}, u32[]{:S(2)}) collective-permute-start(bf16[128,2176]{1,0:T(8,128)(2,1)S(1)} %get-tuple-element.67), channel_id=1, source_target_pairs={{0,16},{1,9},{2,18},{3,11},{4,20},{5,13},{6,22},{7,15},{8,24},{9,1... | collective-permute-start | bytes 1671176 | tf_op jit(solution)/shard_map/ppermute | solution.py:365
  5.5 1.5 %collective-permute-start.3 = (bf16[128,2176]{1,0:T(8,128)(2,1)S(1)}, bf16[128,2176]{1,0:T(8,128)(2,1)S(1)}, u32[]{:S(2)}, u32[]{:S(2)}) collective-permute-start(bf16[128,2176]{1,0:T(8,128)(2,1)S(1)} %get-tuple-element.67), channel_id=1, source_target_pairs={{0,8},{1,17},{2,10},{3,19},{4,12},{5,21},{6,14},{7,23},{8,0},{9,25... | collective-permute-start | bytes 1671176 | tf_op jit(solution)/shard_map/ppermute | solution.py:365
  7.0 6.1 %own.1 = (bf16[1536,768]{1,0:T(8,128)(2,1)S(1)}, bf16[512,512]{1,0:T(8,128)(2,1)S(1)}, bf16[512,512]{1,0:T(8,128)(2,1)S(1)}, f32[256,256]{1,0:T(8,128)S(1)}, bf1...) custom-call(s32[2]{0:T(128)S(1)} %pad_add_fusion.place, ...), custom_call_target="tpu_custom_call" | custom-call | tf_op jit(solution)/shard_map/own/pallas_call | solution.py:410
  13.9 0.8 %sums.4.refs_0_ = f32[1536,768]{1,0:T(8,128)S(1)} custom-call(bf16[256,1536]{1,0:T(8,128)(2,1)S(1)} %get-tuple-element.68.left, bf16[256,768]{1,0:T(8,128)(2,1)S(1)} %get-tuple-element.69.right), custom_call_target="tpu_custom_call" | custom-call | tf_op jit(solution)/shard_map/sums/pallas_call | solution.py:435
  15.1 3.3 %collective-permute-done.2.refs_3_ = bf16[128,2176]{1,0:T(8,128)(2,1)S(1)} collective-permute-done((bf16[128,2176]{1,0:T(8,128)(2,1)S(1)}, bf16[128,2176]{1,0:T(8,128)(2,1)S(1)}, u32[]{:S(2)}, u32[]{:S(2)}) %collective-permute-start.2) | collective-permute-done | bytes 557088 | tf_op jit(solution)/shard_map/ppermute | solution.py:365
  18.4 1.6 %collective-permute-done.3.refs_0_ = bf16[128,2176]{1,0:T(8,128)(2,1)S(1)} collective-permute-done((bf16[128,2176]{1,0:T(8,128)(2,1)S(1)}, bf16[128,2176]{1,0:T(8,128)(2,1)S(1)}, u32[]{:S(2)}, u32[]{:S(2)}) %collective-permute-start.3) | collective-permute-done | bytes 557088 | tf_op jit(solution)/shard_map/ppermute | solution.py:365
  20.6 3.5 %collective-permute-done.5.refs_5_ = bf16[256,512]{1,0:T(8,128)(2,1)S(1)} collective-permute-done((bf16[256,512]{1,0:T(8,128)(2,1)S(1)}, bf16[256,512]{1,0:T(8,128)(2,1)S(1)}, u32[]{:S(2)}, u32[]{:S(2)}) %collective-permute-start.5) | collective-permute-done | bytes 262176 | tf_op jit(solution)/shard_map/ppermute | solution.py:365
  24.1 1.5 %collective-permute-start.8 = (bf16[128,2176]{1,0:T(8,128)(2,1)S(1)}, bf16[128,2176]{1,0:T(8,128)(2,1)S(1)}, u32[]{:S(2)}, u32[]{:S(2)}) collective-permute-start(bf16[128,2176]{1,0:T(8,128)(2,1)S(1)} %collective-permute-done.2.refs_3_), channel_id=1, source_target_pairs={{0,8},{1,17},{2,10},{3,19},{4,12},{5,21},{6,14},{7,23},{8,0},{9,25... | collective-permute-start | bytes 1671176 | tf_op jit(solution)/shard_map/ppermute | solution.py:365
  25.7 1.8 %collective-permute-start.1 = (bf16[64,2176]{1,0:T(8,128)(2,1)S(1)}, bf16[64,2176]{1,0:T(8,128)(2,1)S(1)}, u32[]{:S(2)}, u32[]{:S(2)}) collective-permute-start(bf16[64,2176]{1,0:T(8,128)(2,1)S(1)} %get-tuple-element.66), channel_id=1, source_target_pairs={{0,2},{1,3},{2,0},{3,1},{4,6},{5,7},{6,4},{7,5},{8,10},{9,11},{10,... | collective-permute-start | bytes 835592 | tf_op jit(solution)/shard_map/ppermute | solution.py:348
  27.5 5.3 %far.2 = (bf16[512,1536]{1,0:T(8,128)(2,1)S(1)}, bf16[512,576]{1,0:T(8,128)(2,1)S(1)}, bf16[512,768]{1,0:T(8,128)(2,1)S(1)}, bf16[512,1024]{1,0:T(8,128)(2,1)S(1)}) custom-call(s32[2]{0:T(128)S(1)} %pad_add_fusion.place, bf16[128,2176]{1,0:T(8,128)(2,1)S(1)} %collective-permute-done.3.refs_0_, bf16[128,2176]{1,0:T(8,128)(2,1)S(1)} %collective-permute-done.4.refs_1_, ...), custom_call_target="tpu_custom_call" | custom-call | tf_op jit(solution)/shard_map/far/pallas_call | solution.py:503
  32.8 2.3 %collective-permute-done.1.received = bf16[64,2176]{1,0:T(8,128)(2,1)S(1)} collective-permute-done((bf16[64,2176]{1,0:T(8,128)(2,1)S(1)}, bf16[64,2176]{1,0:T(8,128)(2,1)S(1)}, u32[]{:S(2)}, u32[]{:S(2)}) %collective-permute-start.1) | collective-permute-done | bytes 278560 | tf_op jit(solution)/shard_map/ppermute | solution.py:348
  35.3 2.7 %collective-permute-start.12 = (bf16[32,2176]{1,0:T(8,128)(2,1)S(1)}, bf16[32,2176]{1,0:T(8,128)(2,1)S(1)}, u32[]{:S(2)}, u32[]{:S(2)}) collective-permute-start(bf16[32,2176]{1,0:T(8,128)(2,1)S(1)} %get-tuple-element.106), channel_id=1, source_target_pairs={{0,4},{1,5},{2,6},{3,7},{4,0},{5,1},{6,2},{7,3},{8,12},{9,13},{10,... | collective-permute-start | bytes 417800 | tf_op jit(solution)/shard_map/ppermute | solution.py:348
  38.0 1.9 %sums.7.pq = f32[1536,768]{1,0:T(8,128)S(1)} custom-call(bf16[512,1536]{1,0:T(8,128)(2,1)S(1)} %get-tuple-element.100.left, bf16[512,768]{1,0:T(8,128)(2,1)S(1)} %get-tuple-element.101.right, f32[1536,768]{1,0:T(8,128)S(1)} %sums.4.refs_0_), custom_call_target="tpu_custom_call", output_to_operand_aliasing={{}: (2, {})} | custom-call | tf_op jit(solution)/shard_map/sums/pallas_call | solution.py:435
  39.9 0.8 %sums.6 = (f32[512,512]{1,0:T(8,128)S(1)}, f32[512,512]{1,0:T(8,128)S(1)}) custom-call(bf16[512,576]{1,0:T(8,128)(2,1)S(1)} %get-tuple-element.90.left, bf16[512,1024]{1,0:T(8,128)(2,1)S(1)} %get-tuple-element.91.right, f32[512,512]{1,0:T(8,128)S(1)} %get-tuple-element.92.refs_0_, ...), custom_call_target="tpu_custom_call", output_to_operand_aliasing={{0}: (2, {}), {1}: (3, {})} | custom-call | tf_op jit(solution)/shard_map/sums/pallas_call | solution.py:435
  40.8 0.9 %collective-permute-done.10.refs_2_ = bf16[256,512]{1,0:T(8,128)(2,1)S(1)} collective-permute-done((bf16[256,512]{1,0:T(8,128)(2,1)S(1)}, bf16[256,512]{1,0:T(8,128)(2,1)S(1)}, u32[]{:S(2)}, u32[]{:S(2)}) %collective-permute-start.10) | collective-permute-done | bytes 262176 | tf_op jit(solution)/shard_map/ppermute | solution.py:365
  41.7 3.3 %far.3 = (bf16[256,1536]{1,0:T(8,128)(2,1)S(1)}, bf16[256,576]{1,0:T(8,128)(2,1)S(1)}, bf16[256,768]{1,0:T(8,128)(2,1)S(1)}, bf16[256,1024]{1,0:T(8,128)(2,1)S(1)}) custom-call(s32[2]{0:T(128)S(1)} %pad_add_fusion.place, bf16[128,2176]{1,0:T(8,128)(2,1)S(1)} %collective-permute-done.8.refs_0_, bf16[128,2176]{1,0:T(8,128)(2,1)S(1)} %collective-permute-done.9.refs_1_, ...), custom_call_target="tpu_custom_call" | custom-call | tf_op jit(solution)/shard_map/far/pallas_call | solution.py:503
  45.0 2.0 %last.1 = (f32[1536,768]{1,0:T(8,128)S(1)}, f32[512,512]{1,0:T(8,128)S(1)}, f32[512,512]{1,0:T(8,128)S(1)}, f32[8,128]{1,0:T(8,128)S(1)}) custom-call(bf16[256,1536]{1,0:T(8,128)(2,1)S(1)} %get-tuple-element.96.xq, bf16[256,576]{1,0:T(8,128)(2,1)S(1)} %get-tuple-element.97.xkv, ...), custom_call_target="tpu_custom_call", output_to_operand_aliasing={{0}: (4, {}), {1}: (5, {}), {2}: (6, {})} | custom-call | tf_op jit(solution)/shard_map/last/pallas_call | solution.py:531
  47.1 1.2 %collective-permute-done.11.right = f32[8,128]{1,0:T(8,128)S(1)} collective-permute-done((f32[8,128]{1,0:T(8,128)S(1)}, f32[8,128]{1,0:T(8,128)S(1)}, u32[]{:S(2)}, u32[]{:S(2)}) %collective-permute-start.11) | collective-permute-done | bytes 4128 | tf_op jit(solution)/shard_map/ppermute | solution.py:348
  48.3 1.6 %collective-permute-start.13 = (f32[8,128]{1,0:T(8,128)S(1)}, f32[8,128]{1,0:T(8,128)S(1)}, u32[]{:S(2)}, u32[]{:S(2)}) collective-permute-start(f32[8,128]{1,0:T(8,128)S(1)} %add.9.refs_0_), channel_id=1, source_target_pairs={{0,2},{1,3},{2,0},{3,1},{4,6},{5,7},{6,4},{7,5},{8,10},{9,11},{10,... | collective-permute-start | bytes 12296 | tf_op jit(solution)/shard_map/ppermute | solution.py:348
  49.8 2.6 %collective-permute-start.14 = (f32[8,128]{1,0:T(8,128)S(1)}, f32[8,128]{1,0:T(8,128)S(1)}, u32[]{:S(2)}, u32[]{:S(2)}) collective-permute-start(f32[8,128]{1,0:T(8,128)S(1)} %add.9.refs_0_), channel_id=1, source_target_pairs={{0,4},{1,5},{2,6},{3,7},{4,0},{5,1},{6,2},{7,3},{8,12},{9,13},{10,... | collective-permute-start | bytes 12296 | tf_op jit(solution)/shard_map/ppermute | solution.py:348
  52.7 1.7 %collective-permute-done.14.refs_2_ = f32[8,128]{1,0:T(8,128)S(1)} collective-permute-done((f32[8,128]{1,0:T(8,128)S(1)}, f32[8,128]{1,0:T(8,128)S(1)}, u32[]{:S(2)}, u32[]{:S(2)}) %collective-permute-start.14) | collective-permute-done | bytes 4128 | tf_op jit(solution)/shard_map/ppermute | solution.py:348
  54.4 3.5 %collective-permute-done.15.refs_3_ = f32[8,128]{1,0:T(8,128)S(1)} collective-permute-done((f32[8,128]{1,0:T(8,128)S(1)}, f32[8,128]{1,0:T(8,128)S(1)}, u32[]{:S(2)}, u32[]{:S(2)}) %collective-permute-start.15) | collective-permute-done | bytes 4128 | tf_op jit(solution)/shard_map/ppermute | solution.py:348
  57.8 2.7 %scale.1 = (bf16[1536,768]{1,0:T(8,128)(2,1)}, bf16[512,512]{1,0:T(8,128)(2,1)}, bf16[512,512]{1,0:T(8,128)(2,1)}, f32[32,1536]{1,0:T(8,128)}, f32[32,576]{1,0:T(8,128)}) custom-call(f32[32,2176]{1,0:T(8,128)S(1)} %get-tuple-element.84.local, bf16[32,2176]{1,0:T(8,128)(2,1)S(1)} %collective-permute-done.12.received, f32[1536,768]{1,0:T(8,128)S(1)} %get-tuple-element.108.sq, ...), custom_call_target="tpu_custom_call" | custom-call | tf_op jit(solution)/shard_map/scale/pallas_call | solution.py:547
  (22 shorter events, 2.4 us)
Async XLA Ops:
  2.4 16.0 %collective-permute-start.2 = (bf16[128,2176]{1,0:T(8,128)(2,1)S(1)}, bf16[128,2176]{1,0:T(8,128)(2,1)S(1)}, u32[]{:S(2)}, u32[]{:S(2)}) collective-permute-start(bf16[128,2176]{1,0:T(8,128)(2,1)S(1)} %get-tuple-element.67), channel_id=1, source_target_pairs={{0,16},{1,9},{2,18},{3,11},{4,20},{5,13},{6,22},{7,15},{8,24},{9,1... | collective-permute-start | bytes 1671176 | tf_op jit(solution)/shard_map/ppermute | solution.py:365
  5.5 14.6 %collective-permute-start.3 = (bf16[128,2176]{1,0:T(8,128)(2,1)S(1)}, bf16[128,2176]{1,0:T(8,128)(2,1)S(1)}, u32[]{:S(2)}, u32[]{:S(2)}) collective-permute-start(bf16[128,2176]{1,0:T(8,128)(2,1)S(1)} %get-tuple-element.67), channel_id=1, source_target_pairs={{0,8},{1,17},{2,10},{3,19},{4,12},{5,21},{6,14},{7,23},{8,0},{9,25... | collective-permute-start | bytes 1671176 | tf_op jit(solution)/shard_map/ppermute | solution.py:365
  13.1 12.4 %collective-permute-start = (bf16[128,2176]{1,0:T(8,128)(2,1)S(1)}, bf16[128,2176]{1,0:T(8,128)(2,1)S(1)}, u32[]{:S(2)}, u32[]{:S(2)}) collective-permute-start(bf16[128,2176]{1,0:T(8,128)(2,1)S(1)} %get-tuple-element.64), channel_id=1, source_target_pairs={{0,1},{1,0},{2,3},{3,2},{4,5},{5,4},{6,7},{7,6},{8,9},{9,8},{10,11... | collective-permute-start | bytes 1671176 | tf_op jit(solution)/shard_map/ppermute | solution.py:348
  13.2 10.9 %collective-permute-start.5 = (bf16[256,512]{1,0:T(8,128)(2,1)S(1)}, bf16[256,512]{1,0:T(8,128)(2,1)S(1)}, u32[]{:S(2)}, u32[]{:S(2)}) collective-permute-start(bf16[256,512]{1,0:T(8,128)(2,1)S(1)} %get-tuple-element.75), channel_id=1, source_target_pairs={{0,16},{1,9},{2,18},{3,11},{4,20},{5,13},{6,22},{7,15},{8,24},{9,1... | collective-permute-start | bytes 786440 | tf_op jit(solution)/shard_map/ppermute | solution.py:365
  13.8 10.3 %collective-permute-start.6 = (bf16[256,512]{1,0:T(8,128)(2,1)S(1)}, bf16[256,512]{1,0:T(8,128)(2,1)S(1)}, u32[]{:S(2)}, u32[]{:S(2)}) collective-permute-start(bf16[256,512]{1,0:T(8,128)(2,1)S(1)} %get-tuple-element.75), channel_id=1, source_target_pairs={{0,8},{1,17},{2,10},{3,19},{4,12},{5,21},{6,14},{7,23},{8,0},{9,25... | collective-permute-start | bytes 786440 | tf_op jit(solution)/shard_map/ppermute | solution.py:365
  20.1 7.4 %collective-permute-start.4 = (bf16[128,2176]{1,0:T(8,128)(2,1)S(1)}, bf16[128,2176]{1,0:T(8,128)(2,1)S(1)}, u32[]{:S(2)}, u32[]{:S(2)}) collective-permute-start(bf16[128,2176]{1,0:T(8,128)(2,1)S(1)} %collective-permute-done.2.refs_3_), channel_id=1, source_target_pairs={{0,1},{1,0},{2,3},{3,2},{4,5},{5,4},{6,7},{7,6},{8,9},{9,8},{10,11... | collective-permute-start | bytes 1671176 | tf_op jit(solution)/shard_map/ppermute | solution.py:348
  20.1 7.4 %collective-permute-start.7 = (bf16[128,2176]{1,0:T(8,128)(2,1)S(1)}, bf16[128,2176]{1,0:T(8,128)(2,1)S(1)}, u32[]{:S(2)}, u32[]{:S(2)}) collective-permute-start(bf16[128,2176]{1,0:T(8,128)(2,1)S(1)} %collective-permute-done.3.refs_0_), channel_id=1, source_target_pairs={{0,1},{1,0},{2,3},{3,2},{4,5},{5,4},{6,7},{7,6},{8,9},{9,8},{10,11... | collective-permute-start | bytes 1671176 | tf_op jit(solution)/shard_map/ppermute | solution.py:348
  24.1 11.1 %collective-permute-start.8 = (bf16[128,2176]{1,0:T(8,128)(2,1)S(1)}, bf16[128,2176]{1,0:T(8,128)(2,1)S(1)}, u32[]{:S(2)}, u32[]{:S(2)}) collective-permute-start(bf16[128,2176]{1,0:T(8,128)(2,1)S(1)} %collective-permute-done.2.refs_3_), channel_id=1, source_target_pairs={{0,8},{1,17},{2,10},{3,19},{4,12},{5,21},{6,14},{7,23},{8,0},{9,25... | collective-permute-start | bytes 1671176 | tf_op jit(solution)/shard_map/ppermute | solution.py:365
  25.7 9.5 %collective-permute-start.1 = (bf16[64,2176]{1,0:T(8,128)(2,1)S(1)}, bf16[64,2176]{1,0:T(8,128)(2,1)S(1)}, u32[]{:S(2)}, u32[]{:S(2)}) collective-permute-start(bf16[64,2176]{1,0:T(8,128)(2,1)S(1)} %get-tuple-element.66), channel_id=1, source_target_pairs={{0,2},{1,3},{2,0},{3,1},{4,6},{5,7},{6,4},{7,5},{8,10},{9,11},{10,... | collective-permute-start | bytes 835592 | tf_op jit(solution)/shard_map/ppermute | solution.py:348
  35.2 5.6 %collective-permute-start.9 = (bf16[128,2176]{1,0:T(8,128)(2,1)S(1)}, bf16[128,2176]{1,0:T(8,128)(2,1)S(1)}, u32[]{:S(2)}, u32[]{:S(2)}) collective-permute-start(bf16[128,2176]{1,0:T(8,128)(2,1)S(1)} %collective-permute-done.8.refs_0_), channel_id=1, source_target_pairs={{0,1},{1,0},{2,3},{3,2},{4,5},{5,4},{6,7},{7,6},{8,9},{9,8},{10,11... | collective-permute-start | bytes 1671176 | tf_op jit(solution)/shard_map/ppermute | solution.py:348
  35.3 6.4 %collective-permute-start.10 = (bf16[256,512]{1,0:T(8,128)(2,1)S(1)}, bf16[256,512]{1,0:T(8,128)(2,1)S(1)}, u32[]{:S(2)}, u32[]{:S(2)}) collective-permute-start(bf16[256,512]{1,0:T(8,128)(2,1)S(1)} %collective-permute-done.5.refs_5_), channel_id=1, source_target_pairs={{0,8},{1,17},{2,10},{3,19},{4,12},{5,21},{6,14},{7,23},{8,0},{9,25... | collective-permute-start | bytes 786440 | tf_op jit(solution)/shard_map/ppermute | solution.py:365
  35.3 12.9 %collective-permute-start.12 = (bf16[32,2176]{1,0:T(8,128)(2,1)S(1)}, bf16[32,2176]{1,0:T(8,128)(2,1)S(1)}, u32[]{:S(2)}, u32[]{:S(2)}) collective-permute-start(bf16[32,2176]{1,0:T(8,128)(2,1)S(1)} %get-tuple-element.106), channel_id=1, source_target_pairs={{0,4},{1,5},{2,6},{3,7},{4,0},{5,1},{6,2},{7,3},{8,12},{9,13},{10,... | collective-permute-start | bytes 417800 | tf_op jit(solution)/shard_map/ppermute | solution.py:348
  47.0 1.2 %collective-permute-start.11 = (f32[8,128]{1,0:T(8,128)S(1)}, f32[8,128]{1,0:T(8,128)S(1)}, u32[]{:S(2)}, u32[]{:S(2)}) collective-permute-start(f32[8,128]{1,0:T(8,128)S(1)} %get-tuple-element.105.left), channel_id=1, source_target_pairs={{0,1},{1,0},{2,3},{3,2},{4,5},{5,4},{6,7},{7,6},{8,9},{9,8},{10,11... | collective-permute-start | bytes 12296 | tf_op jit(solution)/shard_map/ppermute | solution.py:348
  48.3 4.4 %collective-permute-start.13 = (f32[8,128]{1,0:T(8,128)S(1)}, f32[8,128]{1,0:T(8,128)S(1)}, u32[]{:S(2)}, u32[]{:S(2)}) collective-permute-start(f32[8,128]{1,0:T(8,128)S(1)} %add.9.refs_0_), channel_id=1, source_target_pairs={{0,2},{1,3},{2,0},{3,1},{4,6},{5,7},{6,4},{7,5},{8,10},{9,11},{10,... | collective-permute-start | bytes 12296 | tf_op jit(solution)/shard_map/ppermute | solution.py:348
  49.8 4.5 %collective-permute-start.14 = (f32[8,128]{1,0:T(8,128)S(1)}, f32[8,128]{1,0:T(8,128)S(1)}, u32[]{:S(2)}, u32[]{:S(2)}) collective-permute-start(f32[8,128]{1,0:T(8,128)S(1)} %add.9.refs_0_), channel_id=1, source_target_pairs={{0,4},{1,5},{2,6},{3,7},{4,0},{5,1},{6,2},{7,3},{8,12},{9,13},{10,... | collective-permute-start | bytes 12296 | tf_op jit(solution)/shard_map/ppermute | solution.py:348
  52.4 5.4 %collective-permute-start.15 = (f32[8,128]{1,0:T(8,128)S(1)}, f32[8,128]{1,0:T(8,128)S(1)}, u32[]{:S(2)}, u32[]{:S(2)}) collective-permute-start(f32[8,128]{1,0:T(8,128)S(1)} %add.9.refs_0_), channel_id=1, source_target_pairs={{0,6},{1,7},{2,4},{3,5},{4,2},{5,3},{6,0},{7,1},{8,14},{9,15},{10,... | collective-permute-start | bytes 12296 | tf_op jit(solution)/shard_map/ppermute | solution.py:348

commit v2 on v1

--- a/solution.py
+++ b/solution.py
@@ -303,23 +303,26 @@
 
 
 def scale_kernel(limit, local, received, sq, sk, sv, *refs):
-    *parts, oq, ok, ov, latent_q, latent_kv, bq, bk, bv, sem = refs
+    *parts, oq, ok, ov, latent_q, latent_kv, bq, bk, bv, bl, br, sem = refs
+    terms = local[...] + received[...].astype(jnp.float32)
+    bl[...] = terms[:, :QL]
+    br[...] = terms[:, QL:LATENT]
+    copies = []
+    for buffer, out in ((bl, latent_q), (br, latent_kv)):
+        copies.append(pltpu.make_async_copy(buffer, out, sem.at[len(copies)]))
+        copies[-1].start()
     total = parts[0][...]
     for part in parts[1:]:
         total = total + part[...]
     total = jnp.sum(total, keepdims=True)
     factor = jnp.minimum(1.0, limit / jnp.sqrt(total + eps))
-    copies = []
     for source, buffer, out in ((sq, bq, oq), (sk, bk, ok), (sv, bv, ov)):
-        for start in range(0, source.shape[0], 256):
-            rows = slice(start, start + 256)
+        for start in range(0, source.shape[0], 128):
+            rows = slice(start, start + 128)
             buffer[rows, :] = (source[rows, :] * factor).astype(jnp.bfloat16)
             copy = pltpu.make_async_copy(buffer.at[rows], out.at[rows], sem.at[len(copies)])
             copy.start()
             copies.append(copy)
-    terms = local[...] + received[...].astype(jnp.float32)
-    latent_q[...] = terms[:, :QL]
-    latent_kv[...] = terms[:, QL:LATENT]
     for copy in copies:
         copy.wait()
 
@@ -517,15 +520,12 @@
         if group is groups[0]:
             came, found[3] = lax.optimization_barrier((came, found[3]))
             stay, go = fold(stay, came)
-            received[k], go, found[2], found[3] = lax.optimization_barrier(
-                (received[k], go, found[2], found[3])
-            )
+            go, found[2] = lax.optimization_barrier((go, found[2]))
             terms = [stay, exchange(go, "head", n_head, bits[-1])]
-        else:
-            received[k], found[2], found[3] = lax.optimization_barrier(
-                (received[k], found[2], found[3])
-            )
         sums[:1] = add_sums(found[0], found[2], sums_shape[:1], sums[:1])
+        received[k], cotangents[k], sums[0] = lax.optimization_barrier(
+            (received[k], cotangents[k], sums[0])
+        )
         sums[1:] = add_sums(found[1], found[3], sums_shape[1:], sums[1:])
 
     *sums, squares = pl.pallas_call(
@@ -552,9 +552,13 @@
             struct((rows, KL + DR), jnp.float32),
         ),
         in_specs=vmem(2 + 3 + len(parts)),
-        out_specs=hbm(3) + vmem(2),
+        out_specs=hbm(5),
         scratch_shapes=list(weights_shape)
-        + [pltpu.SemaphoreType.DMA(((QL + 2 * KL) // 256,))],
+        + [
+            pltpu.VMEM((rows, QL), jnp.float32),
+            pltpu.VMEM((rows, KL + DR), jnp.float32),
+            pltpu.SemaphoreType.DMA((2 + (QL + 2 * KL) // 128,)),
+        ],
         compiler_params=params(),
         cost_estimate=free(),
         name="scale",

time: 60.9 us -> 57.7 us (0.947)
  waiting for transfers between devices: 18 us -> 13.6 us
  starting transfers between devices: 16.3 us -> 18.2 us
    ppermute x10, waiting for transfers between devices: 8.65 us -> 4.57 us  [exchange(): return lax.ppermute(value, axis, [(i, i ^ k) for i in range(size)])]
    ppermute x6, starting transfers between devices: 6.73 us -> 8.19 us  [across(): return lax.ppermute(value, ('dp', 'head'), pairs)]
    pallas_call x1, Pallas kernels: 2.73 us -> 2.09 us  [per_device(): pl.pallas_call(functools.partial(scale_kernel, limit), out_shape=(*[struc...]
  transfers between devices with their start and end apart: 16 -> 16, of which waited for: 8 -> 7; matrix products, arithmetic and copies ran while one was open for 0% -> 0% of each run, Pallas kernels for 35% -> 36%
where the time goes in v2:
time: 57.7 us; the launch traced here: 57.5 us
  Pallas kernels  24.8 us (43%)
  starting transfers between devices  18.2 us (32%)
  waiting for transfers between devices  13.6 us (24%)
  between operations  0.91 us (2%)
    ppermute x10, starting transfers between devices, exchange(): return lax.ppermute(value, axis, [(i, i ^ k) for i in range(size)])  10 us
    ppermute x6, waiting for transfers between devices, across(): return lax.ppermute(value, ('dp', 'head'), pairs)  8.99 us
    pallas_call x2, Pallas kernels, per_device(): pl.pallas_call(functools.partial(far_kernel, n_seq), out_shape=rows_shape...  8.57 us
    ppermute x6, starting transfers between devices, across(): return lax.ppermute(value, ('dp', 'head'), pairs)  8.19 us
    pallas_call x1, Pallas kernels, per_device(): pl.pallas_call(functools.partial(own_kernel, n_head), out_shape=(*weights...  6.13 us
    ppermute x10, waiting for transfers between devices, exchange(): return lax.ppermute(value, axis, [(i, i ^ k) for i in range(size)])  4.57 us
    pallas_call x4, Pallas kernels, add_sums(): pl.pallas_call(functools.partial(sums_kernel, len(shapes), not sums), out...  4.01 us
    pallas_call x1, Pallas kernels, per_device(): pl.pallas_call(functools.partial(scale_kernel, limit), out_shape=(*[struc...  2.09 us
  transfers between devices with their start and end apart: 16, of which 7 were waited for; matrix products, arithmetic and copies ran while one was open for 0% of the time, Pallas kernels for 36%

profile of v2, /device:TPU:0, one launch (start us, length us, event | category | flops | bytes accessed | tf_op | source)
XLA Modules:
  0.0 57.5 jit_solution(14047171994541767522)
XLA Ops:
  0.7 1.7 %load.1 = (bf16[128,2176]{1,0:T(8,128)(2,1)S(1)}, bf16[256,512]{1,0:T(8,128)(2,1)S(1)}) custom-call(s32[2]{0:T(128)S(1)} %pad_add_fusion.place, bf16[256,1536]{1,0:T(8,128)(2,1)} %xq_in.1, bf16[576,256]{1,0:T(8,128)(2,1)} %bitcast.3, bf16[256,512]{1,0:T(8,128)(2,1)} %grad_in.1), custom_call_target="tpu_custom_call" | custom-call | tf_op jit(solution)/shard_map/load/pallas_call | solution.py:383
  2.4 3.0 %collective-permute-start.3 = (bf16[128,2176]{1,0:T(8,128)(2,1)S(1)}, bf16[128,2176]{1,0:T(8,128)(2,1)S(1)}, u32[]{:S(2)}, u32[]{:S(2)}) collective-permute-start(bf16[128,2176]{1,0:T(8,128)(2,1)S(1)} %get-tuple-element.68), channel_id=1, source_target_pairs={{0,8},{1,17},{2,10},{3,19},{4,12},{5,21},{6,14},{7,23},{8,0},{9,25... | collective-permute-start | bytes 1671176 | tf_op jit(solution)/shard_map/ppermute | solution.py:368
  5.5 1.5 %collective-permute-start.2 = (bf16[128,2176]{1,0:T(8,128)(2,1)S(1)}, bf16[128,2176]{1,0:T(8,128)(2,1)S(1)}, u32[]{:S(2)}, u32[]{:S(2)}) collective-permute-start(bf16[128,2176]{1,0:T(8,128)(2,1)S(1)} %get-tuple-element.68), channel_id=1, source_target_pairs={{0,16},{1,9},{2,18},{3,11},{4,20},{5,13},{6,22},{7,15},{8,24},{9,1... | collective-permute-start | bytes 1671176 | tf_op jit(solution)/shard_map/ppermute | solution.py:368
  7.0 6.1 %own.1 = (bf16[1536,768]{1,0:T(8,128)(2,1)S(1)}, bf16[512,512]{1,0:T(8,128)(2,1)S(1)}, bf16[512,512]{1,0:T(8,128)(2,1)S(1)}, f32[256,256]{1,0:T(8,128)S(1)}, bf1...) custom-call(s32[2]{0:T(128)S(1)} %pad_add_fusion.place, ...), custom_call_target="tpu_custom_call" | custom-call | tf_op jit(solution)/shard_map/own/pallas_call | solution.py:413
  13.2 0.6 %collective-permute-start.6 = (bf16[256,512]{1,0:T(8,128)(2,1)S(1)}, bf16[256,512]{1,0:T(8,128)(2,1)S(1)}, u32[]{:S(2)}, u32[]{:S(2)}) collective-permute-start(bf16[256,512]{1,0:T(8,128)(2,1)S(1)} %get-tuple-element.76), channel_id=1, source_target_pairs={{0,8},{1,17},{2,10},{3,19},{4,12},{5,21},{6,14},{7,23},{8,0},{9,25... | collective-permute-start | bytes 786440 | tf_op jit(solution)/shard_map/ppermute | solution.py:368
  14.3 0.8 %sums.4.refs_0_ = f32[1536,768]{1,0:T(8,128)S(1)} custom-call(bf16[256,1536]{1,0:T(8,128)(2,1)S(1)} %get-tuple-element.69.left, bf16[256,768]{1,0:T(8,128)(2,1)S(1)} %get-tuple-element.70.right), custom_call_target="tpu_custom_call" | custom-call | tf_op jit(solution)/shard_map/sums/pallas_call | solution.py:438
  15.1 3.2 %collective-permute-done.3.refs_0_ = bf16[128,2176]{1,0:T(8,128)(2,1)S(1)} collective-permute-done((bf16[128,2176]{1,0:T(8,128)(2,1)S(1)}, bf16[128,2176]{1,0:T(8,128)(2,1)S(1)}, u32[]{:S(2)}, u32[]{:S(2)}) %collective-permute-start.3) | collective-permute-done | bytes 557088 | tf_op jit(solution)/shard_map/ppermute | solution.py:368
  18.4 1.7 %collective-permute-done.2.refs_3_ = bf16[128,2176]{1,0:T(8,128)(2,1)S(1)} collective-permute-done((bf16[128,2176]{1,0:T(8,128)(2,1)S(1)}, bf16[128,2176]{1,0:T(8,128)(2,1)S(1)}, u32[]{:S(2)}, u32[]{:S(2)}) %collective-permute-start.2) | collective-permute-done | bytes 557088 | tf_op jit(solution)/shard_map/ppermute | solution.py:368
  20.6 3.4 %collective-permute-done.6.refs_2_ = bf16[256,512]{1,0:T(8,128)(2,1)S(1)} collective-permute-done((bf16[256,512]{1,0:T(8,128)(2,1)S(1)}, bf16[256,512]{1,0:T(8,128)(2,1)S(1)}, u32[]{:S(2)}, u32[]{:S(2)}) %collective-permute-start.6) | collective-permute-done | bytes 262176 | tf_op jit(solution)/shard_map/ppermute | solution.py:368
  24.0 2.5 %collective-permute-start.8 = (bf16[128,2176]{1,0:T(8,128)(2,1)S(1)}, bf16[128,2176]{1,0:T(8,128)(2,1)S(1)}, u32[]{:S(2)}, u32[]{:S(2)}) collective-permute-start(bf16[128,2176]{1,0:T(8,128)(2,1)S(1)} %collective-permute-done.2.refs_3_), channel_id=1, source_target_pairs={{0,8},{1,17},{2,10},{3,19},{4,12},{5,21},{6,14},{7,23},{8,0},{9,25... | collective-permute-start | bytes 1671176 | tf_op jit(solution)/shard_map/ppermute | solution.py:368
  26.6 1.6 %collective-permute-start.1 = (bf16[64,2176]{1,0:T(8,128)(2,1)S(1)}, bf16[64,2176]{1,0:T(8,128)(2,1)S(1)}, u32[]{:S(2)}, u32[]{:S(2)}) collective-permute-start(bf16[64,2176]{1,0:T(8,128)(2,1)S(1)} %get-tuple-element.67), channel_id=1, source_target_pairs={{0,2},{1,3},{2,0},{3,1},{4,6},{5,7},{6,4},{7,5},{8,10},{9,11},{10,... | collective-permute-start | bytes 835592 | tf_op jit(solution)/shard_map/ppermute | solution.py:351
  28.8 5.3 %far.2 = (bf16[512,1536]{1,0:T(8,128)(2,1)S(1)}, bf16[512,576]{1,0:T(8,128)(2,1)S(1)}, bf16[512,768]{1,0:T(8,128)(2,1)S(1)}, bf16[512,1024]{1,0:T(8,128)(2,1)S(1)}) custom-call(s32[2]{0:T(128)S(1)} %pad_add_fusion.place, bf16[128,2176]{1,0:T(8,128)(2,1)S(1)} %collective-permute-done.3.refs_0_, bf16[128,2176]{1,0:T(8,128)(2,1)S(1)} %collective-permute-done.4.refs_1_, ...), custom_call_target="tpu_custom_call" | custom-call | tf_op jit(solution)/shard_map/far/pallas_call | solution.py:506
  34.2 1.9 %sums.6.pq = f32[1536,768]{1,0:T(8,128)S(1)} custom-call(bf16[512,1536]{1,0:T(8,128)(2,1)S(1)} %get-tuple-element.87.left, bf16[512,768]{1,0:T(8,128)(2,1)S(1)} %get-tuple-element.90.right, f32[1536,768]{1,0:T(8,128)S(1)} %sums.4.refs_0_), custom_call_target="tpu_custom_call", output_to_operand_aliasing={{}: (2, {})} | custom-call | tf_op jit(solution)/shard_map/sums/pallas_call | solution.py:438
  36.2 0.6 %collective-permute-done.9.refs_2_ = bf16[256,512]{1,0:T(8,128)(2,1)S(1)} collective-permute-done((bf16[256,512]{1,0:T(8,128)(2,1)S(1)}, bf16[256,512]{1,0:T(8,128)(2,1)S(1)}, u32[]{:S(2)}, u32[]{:S(2)}) %collective-permute-start.9) | collective-permute-done | bytes 262176 | tf_op jit(solution)/shard_map/ppermute | solution.py:368
  36.8 3.1 %collective-permute-start.12 = (bf16[32,2176]{1,0:T(8,128)(2,1)S(1)}, bf16[32,2176]{1,0:T(8,128)(2,1)S(1)}, u32[]{:S(2)}, u32[]{:S(2)}) collective-permute-start(bf16[32,2176]{1,0:T(8,128)(2,1)S(1)} %get-tuple-element.108), channel_id=1, source_target_pairs={{0,4},{1,5},{2,6},{3,7},{4,0},{5,1},{6,2},{7,3},{8,12},{9,13},{10,... | collective-permute-start | bytes 417800 | tf_op jit(solution)/shard_map/ppermute | solution.py:351
  39.9 0.8 %sums.7 = (f32[512,512]{1,0:T(8,128)S(1)}, f32[512,512]{1,0:T(8,128)S(1)}) custom-call(bf16[512,576]{1,0:T(8,128)(2,1)S(1)} %get-tuple-element.93.left, bf16[512,1024]{1,0:T(8,128)(2,1)S(1)} %get-tuple-element.94.right, f32[512,512]{1,0:T(8,128)S(1)} %get-tuple-element.95.refs_0_, ...), custom_call_target="tpu_custom_call", output_to_operand_aliasing={{0}: (2, {}), {1}: (3, {})} | custom-call | tf_op jit(solution)/shard_map/sums/pallas_call | solution.py:438
  40.7 3.3 %far.3 = (bf16[256,1536]{1,0:T(8,128)(2,1)S(1)}, bf16[256,576]{1,0:T(8,128)(2,1)S(1)}, bf16[256,768]{1,0:T(8,128)(2,1)S(1)}, bf16[256,1024]{1,0:T(8,128)(2,1)S(1)}) custom-call(s32[2]{0:T(128)S(1)} %pad_add_fusion.place, bf16[128,2176]{1,0:T(8,128)(2,1)S(1)} %collective-permute-done.8.refs_0_, bf16[128,2176]{1,0:T(8,128)(2,1)S(1)} %collective-permute-done.10.refs_1_, ...), custom_call_target="tpu_custom_call" | custom-call | tf_op jit(solution)/shard_map/far/pallas_call | solution.py:506
  44.0 2.1 %last.1 = (f32[1536,768]{1,0:T(8,128)S(1)}, f32[512,512]{1,0:T(8,128)S(1)}, f32[512,512]{1,0:T(8,128)S(1)}, f32[8,128]{1,0:T(8,128)S(1)}) custom-call(bf16[256,1536]{1,0:T(8,128)(2,1)S(1)} %get-tuple-element.100.xq, bf16[256,576]{1,0:T(8,128)(2,1)S(1)} %get-tuple-element.101.xkv, ...), custom_call_target="tpu_custom_call", output_to_operand_aliasing={{0}: (4, {}), {1}: (5, {}), {2}: (6, {})} | custom-call | tf_op jit(solution)/shard_map/last/pallas_call | solution.py:531
  46.3 0.9 %collective-permute-done.11.right = f32[8,128]{1,0:T(8,128)S(1)} collective-permute-done((f32[8,128]{1,0:T(8,128)S(1)}, f32[8,128]{1,0:T(8,128)S(1)}, u32[]{:S(2)}, u32[]{:S(2)}) %collective-permute-start.11) | collective-permute-done | bytes 4128 | tf_op jit(solution)/shard_map/ppermute | solution.py:351
  47.3 3.5 %collective-permute-start.15 = (f32[8,128]{1,0:T(8,128)S(1)}, f32[8,128]{1,0:T(8,128)S(1)}, u32[]{:S(2)}, u32[]{:S(2)}) collective-permute-start(f32[8,128]{1,0:T(8,128)S(1)} %add.9.refs_0_), channel_id=1, source_target_pairs={{0,6},{1,7},{2,4},{3,5},{4,2},{5,3},{6,0},{7,1},{8,14},{9,15},{10,... | collective-permute-start | bytes 12296 | tf_op jit(solution)/shard_map/ppermute | solution.py:351
  50.8 0.9 %collective-permute-start.13 = (f32[8,128]{1,0:T(8,128)S(1)}, f32[8,128]{1,0:T(8,128)S(1)}, u32[]{:S(2)}, u32[]{:S(2)}) collective-permute-start(f32[8,128]{1,0:T(8,128)S(1)} %add.9.refs_0_), channel_id=1, source_target_pairs={{0,2},{1,3},{2,0},{3,1},{4,6},{5,7},{6,4},{7,5},{8,10},{9,11},{10,... | collective-permute-start | bytes 12296 | tf_op jit(solution)/shard_map/ppermute | solution.py:351
  51.7 1.0 %collective-permute-done.15.refs_3_ = f32[8,128]{1,0:T(8,128)S(1)} collective-permute-done((f32[8,128]{1,0:T(8,128)S(1)}, f32[8,128]{1,0:T(8,128)S(1)}, u32[]{:S(2)}, u32[]{:S(2)}) %collective-permute-start.15) | collective-permute-done | bytes 4128 | tf_op jit(solution)/shard_map/ppermute | solution.py:351
  52.7 2.6 %collective-permute-done.14.refs_2_ = f32[8,128]{1,0:T(8,128)S(1)} collective-permute-done((f32[8,128]{1,0:T(8,128)S(1)}, f32[8,128]{1,0:T(8,128)S(1)}, u32[]{:S(2)}, u32[]{:S(2)}) %collective-permute-start.14) | collective-permute-done | bytes 4128 | tf_op jit(solution)/shard_map/ppermute | solution.py:351
  55.3 2.1 %scale.1 = (bf16[1536,768]{1,0:T(8,128)(2,1)}, bf16[512,512]{1,0:T(8,128)(2,1)}, bf16[512,512]{1,0:T(8,128)(2,1)}, f32[32,1536]{1,0:T(8,128)}, f32[32,576]{1,0:T(8,128)}) custom-call(f32[32,2176]{1,0:T(8,128)S(1)} %get-tuple-element.85.local, bf16[32,2176]{1,0:T(8,128)(2,1)S(1)} %collective-permute-done.12.received, f32[1536,768]{1,0:T(8,128)S(1)} %get-tuple-element.110.sq, ...), custom_call_target="tpu_custom_call" | custom-call | tf_op jit(solution)/shard_map/scale/pallas_call | solution.py:547
  (22 shorter events, 2.2 us)
Async XLA Ops:
  2.4 15.9 %collective-permute-start.3 = (bf16[128,2176]{1,0:T(8,128)(2,1)S(1)}, bf16[128,2176]{1,0:T(8,128)(2,1)S(1)}, u32[]{:S(2)}, u32[]{:S(2)}) collective-permute-start(bf16[128,2176]{1,0:T(8,128)(2,1)S(1)} %get-tuple-element.68), channel_id=1, source_target_pairs={{0,8},{1,17},{2,10},{3,19},{4,12},{5,21},{6,14},{7,23},{8,0},{9,25... | collective-permute-start | bytes 1671176 | tf_op jit(solution)/shard_map/ppermute | solution.py:368
  5.5 14.6 %collective-permute-start.2 = (bf16[128,2176]{1,0:T(8,128)(2,1)S(1)}, bf16[128,2176]{1,0:T(8,128)(2,1)S(1)}, u32[]{:S(2)}, u32[]{:S(2)}) collective-permute-start(bf16[128,2176]{1,0:T(8,128)(2,1)S(1)} %get-tuple-element.68), channel_id=1, source_target_pairs={{0,16},{1,9},{2,18},{3,11},{4,20},{5,13},{6,22},{7,15},{8,24},{9,1... | collective-permute-start | bytes 1671176 | tf_op jit(solution)/shard_map/ppermute | solution.py:368
  13.1 13.4 %collective-permute-start = (bf16[128,2176]{1,0:T(8,128)(2,1)S(1)}, bf16[128,2176]{1,0:T(8,128)(2,1)S(1)}, u32[]{:S(2)}, u32[]{:S(2)}) collective-permute-start(bf16[128,2176]{1,0:T(8,128)(2,1)S(1)} %get-tuple-element.65), channel_id=1, source_target_pairs={{0,1},{1,0},{2,3},{3,2},{4,5},{5,4},{6,7},{7,6},{8,9},{9,8},{10,11... | collective-permute-start | bytes 1671176 | tf_op jit(solution)/shard_map/ppermute | solution.py:351
  13.2 10.8 %collective-permute-start.6 = (bf16[256,512]{1,0:T(8,128)(2,1)S(1)}, bf16[256,512]{1,0:T(8,128)(2,1)S(1)}, u32[]{:S(2)}, u32[]{:S(2)}) collective-permute-start(bf16[256,512]{1,0:T(8,128)(2,1)S(1)} %get-tuple-element.76), channel_id=1, source_target_pairs={{0,8},{1,17},{2,10},{3,19},{4,12},{5,21},{6,14},{7,23},{8,0},{9,25... | collective-permute-start | bytes 786440 | tf_op jit(solution)/shard_map/ppermute | solution.py:368
  13.8 10.2 %collective-permute-start.5 = (bf16[256,512]{1,0:T(8,128)(2,1)S(1)}, bf16[256,512]{1,0:T(8,128)(2,1)S(1)}, u32[]{:S(2)}, u32[]{:S(2)}) collective-permute-start(bf16[256,512]{1,0:T(8,128)(2,1)S(1)} %get-tuple-element.76), channel_id=1, source_target_pairs={{0,16},{1,9},{2,18},{3,11},{4,20},{5,13},{6,22},{7,15},{8,24},{9,1... | collective-permute-start | bytes 786440 | tf_op jit(solution)/shard_map/ppermute | solution.py:368
  20.1 8.7 %collective-permute-start.7 = (bf16[128,2176]{1,0:T(8,128)(2,1)S(1)}, bf16[128,2176]{1,0:T(8,128)(2,1)S(1)}, u32[]{:S(2)}, u32[]{:S(2)}) collective-permute-start(bf16[128,2176]{1,0:T(8,128)(2,1)S(1)} %collective-permute-done.3.refs_0_), channel_id=1, source_target_pairs={{0,1},{1,0},{2,3},{3,2},{4,5},{5,4},{6,7},{7,6},{8,9},{9,8},{10,11... | collective-permute-start | bytes 1671176 | tf_op jit(solution)/shard_map/ppermute | solution.py:351
  20.1 8.7 %collective-permute-start.4 = (bf16[128,2176]{1,0:T(8,128)(2,1)S(1)}, bf16[128,2176]{1,0:T(8,128)(2,1)S(1)}, u32[]{:S(2)}, u32[]{:S(2)}) collective-permute-start(bf16[128,2176]{1,0:T(8,128)(2,1)S(1)} %collective-permute-done.2.refs_3_), channel_id=1, source_target_pairs={{0,1},{1,0},{2,3},{3,2},{4,5},{5,4},{6,7},{7,6},{8,9},{9,8},{10,11... | collective-permute-start | bytes 1671176 | tf_op jit(solution)/shard_map/ppermute | solution.py:351
  24.0 12.8 %collective-permute-start.8 = (bf16[128,2176]{1,0:T(8,128)(2,1)S(1)}, bf16[128,2176]{1,0:T(8,128)(2,1)S(1)}, u32[]{:S(2)}, u32[]{:S(2)}) collective-permute-start(bf16[128,2176]{1,0:T(8,128)(2,1)S(1)} %collective-permute-done.2.refs_3_), channel_id=1, source_target_pairs={{0,8},{1,17},{2,10},{3,19},{4,12},{5,21},{6,14},{7,23},{8,0},{9,25... | collective-permute-start | bytes 1671176 | tf_op jit(solution)/shard_map/ppermute | solution.py:368
  26.6 7.5 %collective-permute-start.1 = (bf16[64,2176]{1,0:T(8,128)(2,1)S(1)}, bf16[64,2176]{1,0:T(8,128)(2,1)S(1)}, u32[]{:S(2)}, u32[]{:S(2)}) collective-permute-start(bf16[64,2176]{1,0:T(8,128)(2,1)S(1)} %get-tuple-element.67), channel_id=1, source_target_pairs={{0,2},{1,3},{2,0},{3,1},{4,6},{5,7},{6,4},{7,5},{8,10},{9,11},{10,... | collective-permute-start | bytes 835592 | tf_op jit(solution)/shard_map/ppermute | solution.py:351
  28.2 8.5 %collective-permute-start.9 = (bf16[256,512]{1,0:T(8,128)(2,1)S(1)}, bf16[256,512]{1,0:T(8,128)(2,1)S(1)}, u32[]{:S(2)}, u32[]{:S(2)}) collective-permute-start(bf16[256,512]{1,0:T(8,128)(2,1)S(1)} %collective-permute-done.5.refs_5_), channel_id=1, source_target_pairs={{0,8},{1,17},{2,10},{3,19},{4,12},{5,21},{6,14},{7,23},{8,0},{9,25... | collective-permute-start | bytes 786440 | tf_op jit(solution)/shard_map/ppermute | solution.py:368
  36.8 3.9 %collective-permute-start.10 = (bf16[128,2176]{1,0:T(8,128)(2,1)S(1)}, bf16[128,2176]{1,0:T(8,128)(2,1)S(1)}, u32[]{:S(2)}, u32[]{:S(2)}) collective-permute-start(bf16[128,2176]{1,0:T(8,128)(2,1)S(1)} %collective-permute-done.8.refs_0_), channel_id=1, source_target_pairs={{0,1},{1,0},{2,3},{3,2},{4,5},{5,4},{6,7},{7,6},{8,9},{9,8},{10,11... | collective-permute-start | bytes 1671176 | tf_op jit(solution)/shard_map/ppermute | solution.py:351
  36.8 10.5 %collective-permute-start.12 = (bf16[32,2176]{1,0:T(8,128)(2,1)S(1)}, bf16[32,2176]{1,0:T(8,128)(2,1)S(1)}, u32[]{:S(2)}, u32[]{:S(2)}) collective-permute-start(bf16[32,2176]{1,0:T(8,128)(2,1)S(1)} %get-tuple-element.108), channel_id=1, source_target_pairs={{0,4},{1,5},{2,6},{3,7},{4,0},{5,1},{6,2},{7,3},{8,12},{9,13},{10,... | collective-permute-start | bytes 417800 | tf_op jit(solution)/shard_map/ppermute | solution.py:351
  46.0 1.2 %collective-permute-start.11 = (f32[8,128]{1,0:T(8,128)S(1)}, f32[8,128]{1,0:T(8,128)S(1)}, u32[]{:S(2)}, u32[]{:S(2)}) collective-permute-start(f32[8,128]{1,0:T(8,128)S(1)} %get-tuple-element.107.left), channel_id=1, source_target_pairs={{0,1},{1,0},{2,3},{3,2},{4,5},{5,4},{6,7},{7,6},{8,9},{9,8},{10,11... | collective-permute-start | bytes 12296 | tf_op jit(solution)/shard_map/ppermute | solution.py:351
  47.3 5.4 %collective-permute-start.15 = (f32[8,128]{1,0:T(8,128)S(1)}, f32[8,128]{1,0:T(8,128)S(1)}, u32[]{:S(2)}, u32[]{:S(2)}) collective-permute-start(f32[8,128]{1,0:T(8,128)S(1)} %add.9.refs_0_), channel_id=1, source_target_pairs={{0,6},{1,7},{2,4},{3,5},{4,2},{5,3},{6,0},{7,1},{8,14},{9,15},{10,... | collective-permute-start | bytes 12296 | tf_op jit(solution)/shard_map/ppermute | solution.py:351
  50.8 4.5 %collective-permute-start.14 = (f32[8,128]{1,0:T(8,128)S(1)}, f32[8,128]{1,0:T(8,128)S(1)}, u32[]{:S(2)}, u32[]{:S(2)}) collective-permute-start(f32[8,128]{1,0:T(8,128)S(1)} %add.9.refs_0_), channel_id=1, source_target_pairs={{0,4},{1,5},{2,6},{3,7},{4,0},{5,1},{6,2},{7,3},{8,12},{9,13},{10,... | collective-permute-start | bytes 12296 | tf_op jit(solution)/shard_map/ppermute | solution.py:351
  50.8 4.5 %collective-permute-start.13 = (f32[8,128]{1,0:T(8,128)S(1)}, f32[8,128]{1,0:T(8,128)S(1)}, u32[]{:S(2)}, u32[]{:S(2)}) collective-permute-start(f32[8,128]{1,0:T(8,128)S(1)} %add.9.refs_0_), channel_id=1, source_target_pairs={{0,2},{1,3},{2,0},{3,1},{4,6},{5,7},{6,4},{7,5},{8,10},{9,11},{10,... | collective-permute-start | bytes 12296 | tf_op jit(solution)/shard_map/ppermute | solution.py:351

commit v3 on v2

--- a/solution.py
+++ b/solution.py
@@ -145,13 +145,10 @@
         )
 
     rot_sums = [jnp.zeros((length, TILE), jnp.float32) for _ in spans]
-    pending = first_products(*items[0])
-    even_part = None
-    for index, (span, head) in enumerate(items):
-        products = pending
-        if index + 1 < len(items):
-            pending = first_products(*items[index + 1])
-        probs, grad_scores = softmax_grads(*products)
+    even_parts = {}
+
+    def last_products(index, probs, grad_scores):
+        span, head = items[index]
         query_window, key_window, columns = windows(span, head)
         gkv[span, wide + head * DN : wide + (head + 1) * DN] = dot(probs, grad[span, columns]).astype(
             jnp.bfloat16
@@ -163,14 +160,15 @@
             gkv[span, columns] = key_part[:, :TILE].astype(jnp.bfloat16)
             if rot_out is not None:
                 rot_sums[seq] = rot_sums[seq] + rounded(key_part[:, TILE:])
-            even_part = query_part
-            continue
+            even_parts[index + 1] = query_part
+            return
         turned = pltpu.roll(key_part[:, TILE:], DR, 1)
         gkv[span, columns] = jnp.where(low, pltpu.roll(key_part[:, :TILE], DR, 1), turned).astype(
             jnp.bfloat16
         )
         if rot_out is not None:
             rot_sums[seq] = rot_sums[seq] + rounded(turned)
+        even_part = even_parts.pop(index)
         parts = [
             even_part[:, :TILE],
             even_part[:, TILE:] + query_part[:, :TILE],
@@ -183,6 +181,17 @@
                 part = part * cos_tiles[i - 1] - swap_halves(part) * sin_tiles[i - 1]
             start = PAIR * (head // 2) + i * TILE
             gq[span, start : start + TILE] = part.astype(jnp.bfloat16)
+
+    ahead = [first_products(*item) for item in items[:2]]
+    waiting = None
+    for index in range(len(items)):
+        found = softmax_grads(*ahead.pop(0))
+        if index + 2 < len(items):
+            ahead.append(first_products(*items[index + 2]))
+        if waiting is not None:
+            last_products(index - 1, *waiting)
+        waiting = found
+    last_products(len(items) - 1, *waiting)
     if rot_out is not None:
         rot_out[...] = rot_sums[0]
 

time: 57.7 us -> 57.7 us (level)
  no operation moved by 1% of the time
where the time goes in v3:
time: 57.7 us; the launch traced here: 57.5 us
  Pallas kernels  24.6 us (43%)
  starting transfers between devices  18.2 us (32%)
  waiting for transfers between devices  13.7 us (24%)
  between operations  0.91 us (2%)
    ppermute x10, starting transfers between devices, exchange(): return lax.ppermute(value, axis, [(i, i ^ k) for i in range(size)])  10 us
    ppermute x6, waiting for transfers between devices, across(): return lax.ppermute(value, ('dp', 'head'), pairs)  9.11 us
    pallas_call x2, Pallas kernels, per_device(): pl.pallas_call(functools.partial(far_kernel, n_seq), out_shape=rows_shape...  8.45 us
    ppermute x6, starting transfers between devices, across(): return lax.ppermute(value, ('dp', 'head'), pairs)  8.19 us
    pallas_call x1, Pallas kernels, per_device(): pl.pallas_call(functools.partial(own_kernel, n_head), out_shape=(*weights...  6.09 us
    ppermute x10, waiting for transfers between devices, exchange(): return lax.ppermute(value, axis, [(i, i ^ k) for i in range(size)])  4.61 us
    pallas_call x4, Pallas kernels, add_sums(): pl.pallas_call(functools.partial(sums_kernel, len(shapes), not sums), out...  4.02 us
    pallas_call x1, Pallas kernels, per_device(): pl.pallas_call(functools.partial(scale_kernel, limit), out_shape=(*[struc...  2.09 us
  transfers between devices with their start and end apart: 16, of which 7 were waited for; matrix products, arithmetic and copies ran while one was open for 0% of the time, Pallas kernels for 36%

profile of v3, /device:TPU:0, one launch (start us, length us, event | category | flops | bytes accessed | tf_op | source)
XLA Modules:
  0.0 57.5 jit_solution(5774896493473561082)
XLA Ops:
  0.7 1.7 %load.1 = (bf16[128,2176]{1,0:T(8,128)(2,1)S(1)}, bf16[256,512]{1,0:T(8,128)(2,1)S(1)}) custom-call(s32[2]{0:T(128)S(1)} %pad_add_fusion.place, bf16[256,1536]{1,0:T(8,128)(2,1)} %xq_in.1, bf16[576,256]{1,0:T(8,128)(2,1)} %bitcast.3, bf16[256,512]{1,0:T(8,128)(2,1)} %grad_in.1), custom_call_target="tpu_custom_call" | custom-call | tf_op jit(solution)/shard_map/load/pallas_call | solution.py:392
  2.4 3.0 %collective-permute-start.3 = (bf16[128,2176]{1,0:T(8,128)(2,1)S(1)}, bf16[128,2176]{1,0:T(8,128)(2,1)S(1)}, u32[]{:S(2)}, u32[]{:S(2)}) collective-permute-start(bf16[128,2176]{1,0:T(8,128)(2,1)S(1)} %get-tuple-element.68), channel_id=1, source_target_pairs={{0,8},{1,17},{2,10},{3,19},{4,12},{5,21},{6,14},{7,23},{8,0},{9,25... | collective-permute-start | bytes 1671176 | tf_op jit(solution)/shard_map/ppermute | solution.py:377
  5.5 1.5 %collective-permute-start.2 = (bf16[128,2176]{1,0:T(8,128)(2,1)S(1)}, bf16[128,2176]{1,0:T(8,128)(2,1)S(1)}, u32[]{:S(2)}, u32[]{:S(2)}) collective-permute-start(bf16[128,2176]{1,0:T(8,128)(2,1)S(1)} %get-tuple-element.68), channel_id=1, source_target_pairs={{0,16},{1,9},{2,18},{3,11},{4,20},{5,13},{6,22},{7,15},{8,24},{9,1... | collective-permute-start | bytes 1671176 | tf_op jit(solution)/shard_map/ppermute | solution.py:377
  7.0 6.1 %own.1 = (bf16[1536,768]{1,0:T(8,128)(2,1)S(1)}, bf16[512,512]{1,0:T(8,128)(2,1)S(1)}, bf16[512,512]{1,0:T(8,128)(2,1)S(1)}, f32[256,256]{1,0:T(8,128)S(1)}, bf1...) custom-call(s32[2]{0:T(128)S(1)} %pad_add_fusion.place, ...), custom_call_target="tpu_custom_call" | custom-call | tf_op jit(solution)/shard_map/own/pallas_call | solution.py:422
  13.1 0.6 %collective-permute-start.6 = (bf16[256,512]{1,0:T(8,128)(2,1)S(1)}, bf16[256,512]{1,0:T(8,128)(2,1)S(1)}, u32[]{:S(2)}, u32[]{:S(2)}) collective-permute-start(bf16[256,512]{1,0:T(8,128)(2,1)S(1)} %get-tuple-element.76), channel_id=1, source_target_pairs={{0,8},{1,17},{2,10},{3,19},{4,12},{5,21},{6,14},{7,23},{8,0},{9,25... | collective-permute-start | bytes 786440 | tf_op jit(solution)/shard_map/ppermute | solution.py:377
  14.3 0.8 %sums.4.refs_0_ = f32[1536,768]{1,0:T(8,128)S(1)} custom-call(bf16[256,1536]{1,0:T(8,128)(2,1)S(1)} %get-tuple-element.69.left, bf16[256,768]{1,0:T(8,128)(2,1)S(1)} %get-tuple-element.70.right), custom_call_target="tpu_custom_call" | custom-call | tf_op jit(solution)/shard_map/sums/pallas_call | solution.py:447
  15.1 3.3 %collective-permute-done.3.refs_0_ = bf16[128,2176]{1,0:T(8,128)(2,1)S(1)} collective-permute-done((bf16[128,2176]{1,0:T(8,128)(2,1)S(1)}, bf16[128,2176]{1,0:T(8,128)(2,1)S(1)}, u32[]{:S(2)}, u32[]{:S(2)}) %collective-permute-start.3) | collective-permute-done | bytes 557088 | tf_op jit(solution)/shard_map/ppermute | solution.py:377
  18.4 1.7 %collective-permute-done.2.refs_3_ = bf16[128,2176]{1,0:T(8,128)(2,1)S(1)} collective-permute-done((bf16[128,2176]{1,0:T(8,128)(2,1)S(1)}, bf16[128,2176]{1,0:T(8,128)(2,1)S(1)}, u32[]{:S(2)}, u32[]{:S(2)}) %collective-permute-start.2) | collective-permute-done | bytes 557088 | tf_op jit(solution)/shard_map/ppermute | solution.py:377
  20.6 3.4 %collective-permute-done.6.refs_2_ = bf16[256,512]{1,0:T(8,128)(2,1)S(1)} collective-permute-done((bf16[256,512]{1,0:T(8,128)(2,1)S(1)}, bf16[256,512]{1,0:T(8,128)(2,1)S(1)}, u32[]{:S(2)}, u32[]{:S(2)}) %collective-permute-start.6) | collective-permute-done | bytes 262176 | tf_op jit(solution)/shard_map/ppermute | solution.py:377
  24.0 2.5 %collective-permute-start.8 = (bf16[128,2176]{1,0:T(8,128)(2,1)S(1)}, bf16[128,2176]{1,0:T(8,128)(2,1)S(1)}, u32[]{:S(2)}, u32[]{:S(2)}) collective-permute-start(bf16[128,2176]{1,0:T(8,128)(2,1)S(1)} %collective-permute-done.2.refs_3_), channel_id=1, source_target_pairs={{0,8},{1,17},{2,10},{3,19},{4,12},{5,21},{6,14},{7,23},{8,0},{9,25... | collective-permute-start | bytes 1671176 | tf_op jit(solution)/shard_map/ppermute | solution.py:377
  26.6 1.6 %collective-permute-start.1 = (bf16[64,2176]{1,0:T(8,128)(2,1)S(1)}, bf16[64,2176]{1,0:T(8,128)(2,1)S(1)}, u32[]{:S(2)}, u32[]{:S(2)}) collective-permute-start(bf16[64,2176]{1,0:T(8,128)(2,1)S(1)} %get-tuple-element.67), channel_id=1, source_target_pairs={{0,2},{1,3},{2,0},{3,1},{4,6},{5,7},{6,4},{7,5},{8,10},{9,11},{10,... | collective-permute-start | bytes 835592 | tf_op jit(solution)/shard_map/ppermute | solution.py:360
  28.8 5.2 %far.2 = (bf16[512,1536]{1,0:T(8,128)(2,1)S(1)}, bf16[512,576]{1,0:T(8,128)(2,1)S(1)}, bf16[512,768]{1,0:T(8,128)(2,1)S(1)}, bf16[512,1024]{1,0:T(8,128)(2,1)S(1)}) custom-call(s32[2]{0:T(128)S(1)} %pad_add_fusion.place, bf16[128,2176]{1,0:T(8,128)(2,1)S(1)} %collective-permute-done.3.refs_0_, bf16[128,2176]{1,0:T(8,128)(2,1)S(1)} %collective-permute-done.4.refs_1_, ...), custom_call_target="tpu_custom_call" | custom-call | tf_op jit(solution)/shard_map/far/pallas_call | solution.py:515
  34.1 1.9 %sums.6.pq = f32[1536,768]{1,0:T(8,128)S(1)} custom-call(bf16[512,1536]{1,0:T(8,128)(2,1)S(1)} %get-tuple-element.87.left, bf16[512,768]{1,0:T(8,128)(2,1)S(1)} %get-tuple-element.90.right, f32[1536,768]{1,0:T(8,128)S(1)} %sums.4.refs_0_), custom_call_target="tpu_custom_call", output_to_operand_aliasing={{}: (2, {})} | custom-call | tf_op jit(solution)/shard_map/sums/pallas_call | solution.py:447
  36.1 0.7 %collective-permute-done.9.refs_2_ = bf16[256,512]{1,0:T(8,128)(2,1)S(1)} collective-permute-done((bf16[256,512]{1,0:T(8,128)(2,1)S(1)}, bf16[256,512]{1,0:T(8,128)(2,1)S(1)}, u32[]{:S(2)}, u32[]{:S(2)}) %collective-permute-start.9) | collective-permute-done | bytes 262176 | tf_op jit(solution)/shard_map/ppermute | solution.py:377
  36.8 3.1 %collective-permute-start.12 = (bf16[32,2176]{1,0:T(8,128)(2,1)S(1)}, bf16[32,2176]{1,0:T(8,128)(2,1)S(1)}, u32[]{:S(2)}, u32[]{:S(2)}) collective-permute-start(bf16[32,2176]{1,0:T(8,128)(2,1)S(1)} %get-tuple-element.108), channel_id=1, source_target_pairs={{0,4},{1,5},{2,6},{3,7},{4,0},{5,1},{6,2},{7,3},{8,12},{9,13},{10,... | collective-permute-start | bytes 417800 | tf_op jit(solution)/shard_map/ppermute | solution.py:360
  39.9 0.8 %sums.7 = (f32[512,512]{1,0:T(8,128)S(1)}, f32[512,512]{1,0:T(8,128)S(1)}) custom-call(bf16[512,576]{1,0:T(8,128)(2,1)S(1)} %get-tuple-element.93.left, bf16[512,1024]{1,0:T(8,128)(2,1)S(1)} %get-tuple-element.94.right, f32[512,512]{1,0:T(8,128)S(1)} %get-tuple-element.95.refs_0_, ...), custom_call_target="tpu_custom_call", output_to_operand_aliasing={{0}: (2, {}), {1}: (3, {})} | custom-call | tf_op jit(solution)/shard_map/sums/pallas_call | solution.py:447
  40.7 3.2 %far.3 = (bf16[256,1536]{1,0:T(8,128)(2,1)S(1)}, bf16[256,576]{1,0:T(8,128)(2,1)S(1)}, bf16[256,768]{1,0:T(8,128)(2,1)S(1)}, bf16[256,1024]{1,0:T(8,128)(2,1)S(1)}) custom-call(s32[2]{0:T(128)S(1)} %pad_add_fusion.place, bf16[128,2176]{1,0:T(8,128)(2,1)S(1)} %collective-permute-done.8.refs_0_, bf16[128,2176]{1,0:T(8,128)(2,1)S(1)} %collective-permute-done.10.refs_1_, ...), custom_call_target="tpu_custom_call" | custom-call | tf_op jit(solution)/shard_map/far/pallas_call | solution.py:515
  43.9 2.0 %last.1 = (f32[1536,768]{1,0:T(8,128)S(1)}, f32[512,512]{1,0:T(8,128)S(1)}, f32[512,512]{1,0:T(8,128)S(1)}, f32[8,128]{1,0:T(8,128)S(1)}) custom-call(bf16[256,1536]{1,0:T(8,128)(2,1)S(1)} %get-tuple-element.100.xq, bf16[256,576]{1,0:T(8,128)(2,1)S(1)} %get-tuple-element.101.xkv, ...), custom_call_target="tpu_custom_call", output_to_operand_aliasing={{0}: (4, {}), {1}: (5, {}), {2}: (6, {})} | custom-call | tf_op jit(solution)/shard_map/last/pallas_call | solution.py:540
  46.3 0.9 %collective-permute-done.11.right = f32[8,128]{1,0:T(8,128)S(1)} collective-permute-done((f32[8,128]{1,0:T(8,128)S(1)}, f32[8,128]{1,0:T(8,128)S(1)}, u32[]{:S(2)}, u32[]{:S(2)}) %collective-permute-start.11) | collective-permute-done | bytes 4128 | tf_op jit(solution)/shard_map/ppermute | solution.py:360
  47.2 3.5 %collective-permute-start.15 = (f32[8,128]{1,0:T(8,128)S(1)}, f32[8,128]{1,0:T(8,128)S(1)}, u32[]{:S(2)}, u32[]{:S(2)}) collective-permute-start(f32[8,128]{1,0:T(8,128)S(1)} %add.9.refs_0_), channel_id=1, source_target_pairs={{0,6},{1,7},{2,4},{3,5},{4,2},{5,3},{6,0},{7,1},{8,14},{9,15},{10,... | collective-permute-start | bytes 12296 | tf_op jit(solution)/shard_map/ppermute | solution.py:360
  50.8 0.8 %collective-permute-start.13 = (f32[8,128]{1,0:T(8,128)S(1)}, f32[8,128]{1,0:T(8,128)S(1)}, u32[]{:S(2)}, u32[]{:S(2)}) collective-permute-start(f32[8,128]{1,0:T(8,128)S(1)} %add.9.refs_0_), channel_id=1, source_target_pairs={{0,2},{1,3},{2,0},{3,1},{4,6},{5,7},{6,4},{7,5},{8,10},{9,11},{10,... | collective-permute-start | bytes 12296 | tf_op jit(solution)/shard_map/ppermute | solution.py:360
  51.6 1.0 %collective-permute-done.15.refs_3_ = f32[8,128]{1,0:T(8,128)S(1)} collective-permute-done((f32[8,128]{1,0:T(8,128)S(1)}, f32[8,128]{1,0:T(8,128)S(1)}, u32[]{:S(2)}, u32[]{:S(2)}) %collective-permute-start.15) | collective-permute-done | bytes 4128 | tf_op jit(solution)/shard_map/ppermute | solution.py:360
  52.6 2.6 %collective-permute-done.14.refs_2_ = f32[8,128]{1,0:T(8,128)S(1)} collective-permute-done((f32[8,128]{1,0:T(8,128)S(1)}, f32[8,128]{1,0:T(8,128)S(1)}, u32[]{:S(2)}, u32[]{:S(2)}) %collective-permute-start.14) | collective-permute-done | bytes 4128 | tf_op jit(solution)/shard_map/ppermute | solution.py:360
  55.3 2.1 %scale.1 = (bf16[1536,768]{1,0:T(8,128)(2,1)}, bf16[512,512]{1,0:T(8,128)(2,1)}, bf16[512,512]{1,0:T(8,128)(2,1)}, f32[32,1536]{1,0:T(8,128)}, f32[32,576]{1,0:T(8,128)}) custom-call(f32[32,2176]{1,0:T(8,128)S(1)} %get-tuple-element.85.local, bf16[32,2176]{1,0:T(8,128)(2,1)S(1)} %collective-permute-done.12.received, f32[1536,768]{1,0:T(8,128)S(1)} %get-tuple-element.110.sq, ...), custom_call_target="tpu_custom_call" | custom-call | tf_op jit(solution)/shard_map/scale/pallas_call | solution.py:556
  (22 shorter events, 2.2 us)
Async XLA Ops:
  2.4 15.9 %collective-permute-start.3 = (bf16[128,2176]{1,0:T(8,128)(2,1)S(1)}, bf16[128,2176]{1,0:T(8,128)(2,1)S(1)}, u32[]{:S(2)}, u32[]{:S(2)}) collective-permute-start(bf16[128,2176]{1,0:T(8,128)(2,1)S(1)} %get-tuple-element.68), channel_id=1, source_target_pairs={{0,8},{1,17},{2,10},{3,19},{4,12},{5,21},{6,14},{7,23},{8,0},{9,25... | collective-permute-start | bytes 1671176 | tf_op jit(solution)/shard_map/ppermute | solution.py:377
  5.5 14.6 %collective-permute-start.2 = (bf16[128,2176]{1,0:T(8,128)(2,1)S(1)}, bf16[128,2176]{1,0:T(8,128)(2,1)S(1)}, u32[]{:S(2)}, u32[]{:S(2)}) collective-permute-start(bf16[128,2176]{1,0:T(8,128)(2,1)S(1)} %get-tuple-element.68), channel_id=1, source_target_pairs={{0,16},{1,9},{2,18},{3,11},{4,20},{5,13},{6,22},{7,15},{8,24},{9,1... | collective-permute-start | bytes 1671176 | tf_op jit(solution)/shard_map/ppermute | solution.py:377
  13.1 13.4 %collective-permute-start = (bf16[128,2176]{1,0:T(8,128)(2,1)S(1)}, bf16[128,2176]{1,0:T(8,128)(2,1)S(1)}, u32[]{:S(2)}, u32[]{:S(2)}) collective-permute-start(bf16[128,2176]{1,0:T(8,128)(2,1)S(1)} %get-tuple-element.65), channel_id=1, source_target_pairs={{0,1},{1,0},{2,3},{3,2},{4,5},{5,4},{6,7},{7,6},{8,9},{9,8},{10,11... | collective-permute-start | bytes 1671176 | tf_op jit(solution)/shard_map/ppermute | solution.py:360
  13.1 10.8 %collective-permute-start.6 = (bf16[256,512]{1,0:T(8,128)(2,1)S(1)}, bf16[256,512]{1,0:T(8,128)(2,1)S(1)}, u32[]{:S(2)}, u32[]{:S(2)}) collective-permute-start(bf16[256,512]{1,0:T(8,128)(2,1)S(1)} %get-tuple-element.76), channel_id=1, source_target_pairs={{0,8},{1,17},{2,10},{3,19},{4,12},{5,21},{6,14},{7,23},{8,0},{9,25... | collective-permute-start | bytes 786440 | tf_op jit(solution)/shard_map/ppermute | solution.py:377
  13.7 10.2 %collective-permute-start.5 = (bf16[256,512]{1,0:T(8,128)(2,1)S(1)}, bf16[256,512]{1,0:T(8,128)(2,1)S(1)}, u32[]{:S(2)}, u32[]{:S(2)}) collective-permute-start(bf16[256,512]{1,0:T(8,128)(2,1)S(1)} %get-tuple-element.76), channel_id=1, source_target_pairs={{0,16},{1,9},{2,18},{3,11},{4,20},{5,13},{6,22},{7,15},{8,24},{9,1... | collective-permute-start | bytes 786440 | tf_op jit(solution)/shard_map/ppermute | solution.py:377
  20.1 8.7 %collective-permute-start.7 = (bf16[128,2176]{1,0:T(8,128)(2,1)S(1)}, bf16[128,2176]{1,0:T(8,128)(2,1)S(1)}, u32[]{:S(2)}, u32[]{:S(2)}) collective-permute-start(bf16[128,2176]{1,0:T(8,128)(2,1)S(1)} %collective-permute-done.3.refs_0_), channel_id=1, source_target_pairs={{0,1},{1,0},{2,3},{3,2},{4,5},{5,4},{6,7},{7,6},{8,9},{9,8},{10,11... | collective-permute-start | bytes 1671176 | tf_op jit(solution)/shard_map/ppermute | solution.py:360
  20.1 8.7 %collective-permute-start.4 = (bf16[128,2176]{1,0:T(8,128)(2,1)S(1)}, bf16[128,2176]{1,0:T(8,128)(2,1)S(1)}, u32[]{:S(2)}, u32[]{:S(2)}) collective-permute-start(bf16[128,2176]{1,0:T(8,128)(2,1)S(1)} %collective-permute-done.2.refs_3_), channel_id=1, source_target_pairs={{0,1},{1,0},{2,3},{3,2},{4,5},{5,4},{6,7},{7,6},{8,9},{9,8},{10,11... | collective-permute-start | bytes 1671176 | tf_op jit(solution)/shard_map/ppermute | solution.py:360
  24.0 12.8 %collective-permute-start.8 = (bf16[128,2176]{1,0:T(8,128)(2,1)S(1)}, bf16[128,2176]{1,0:T(8,128)(2,1)S(1)}, u32[]{:S(2)}, u32[]{:S(2)}) collective-permute-start(bf16[128,2176]{1,0:T(8,128)(2,1)S(1)} %collective-permute-done.2.refs_3_), channel_id=1, source_target_pairs={{0,8},{1,17},{2,10},{3,19},{4,12},{5,21},{6,14},{7,23},{8,0},{9,25... | collective-permute-start | bytes 1671176 | tf_op jit(solution)/shard_map/ppermute | solution.py:377
  26.6 7.4 %collective-permute-start.1 = (bf16[64,2176]{1,0:T(8,128)(2,1)S(1)}, bf16[64,2176]{1,0:T(8,128)(2,1)S(1)}, u32[]{:S(2)}, u32[]{:S(2)}) collective-permute-start(bf16[64,2176]{1,0:T(8,128)(2,1)S(1)} %get-tuple-element.67), channel_id=1, source_target_pairs={{0,2},{1,3},{2,0},{3,1},{4,6},{5,7},{6,4},{7,5},{8,10},{9,11},{10,... | collective-permute-start | bytes 835592 | tf_op jit(solution)/shard_map/ppermute | solution.py:360
  28.2 8.5 %collective-permute-start.9 = (bf16[256,512]{1,0:T(8,128)(2,1)S(1)}, bf16[256,512]{1,0:T(8,128)(2,1)S(1)}, u32[]{:S(2)}, u32[]{:S(2)}) collective-permute-start(bf16[256,512]{1,0:T(8,128)(2,1)S(1)} %collective-permute-done.5.refs_5_), channel_id=1, source_target_pairs={{0,8},{1,17},{2,10},{3,19},{4,12},{5,21},{6,14},{7,23},{8,0},{9,25... | collective-permute-start | bytes 786440 | tf_op jit(solution)/shard_map/ppermute | solution.py:377
  36.8 3.9 %collective-permute-start.10 = (bf16[128,2176]{1,0:T(8,128)(2,1)S(1)}, bf16[128,2176]{1,0:T(8,128)(2,1)S(1)}, u32[]{:S(2)}, u32[]{:S(2)}) collective-permute-start(bf16[128,2176]{1,0:T(8,128)(2,1)S(1)} %collective-permute-done.8.refs_0_), channel_id=1, source_target_pairs={{0,1},{1,0},{2,3},{3,2},{4,5},{5,4},{6,7},{7,6},{8,9},{9,8},{10,11... | collective-permute-start | bytes 1671176 | tf_op jit(solution)/shard_map/ppermute | solution.py:360
  36.8 10.4 %collective-permute-start.12 = (bf16[32,2176]{1,0:T(8,128)(2,1)S(1)}, bf16[32,2176]{1,0:T(8,128)(2,1)S(1)}, u32[]{:S(2)}, u32[]{:S(2)}) collective-permute-start(bf16[32,2176]{1,0:T(8,128)(2,1)S(1)} %get-tuple-element.108), channel_id=1, source_target_pairs={{0,4},{1,5},{2,6},{3,7},{4,0},{5,1},{6,2},{7,3},{8,12},{9,13},{10,... | collective-permute-start | bytes 417800 | tf_op jit(solution)/shard_map/ppermute | solution.py:360
  46.0 1.2 %collective-permute-start.11 = (f32[8,128]{1,0:T(8,128)S(1)}, f32[8,128]{1,0:T(8,128)S(1)}, u32[]{:S(2)}, u32[]{:S(2)}) collective-permute-start(f32[8,128]{1,0:T(8,128)S(1)} %get-tuple-element.107.left), channel_id=1, source_target_pairs={{0,1},{1,0},{2,3},{3,2},{4,5},{5,4},{6,7},{7,6},{8,9},{9,8},{10,11... | collective-permute-start | bytes 12296 | tf_op jit(solution)/shard_map/ppermute | solution.py:360
  47.2 5.4 %collective-permute-start.15 = (f32[8,128]{1,0:T(8,128)S(1)}, f32[8,128]{1,0:T(8,128)S(1)}, u32[]{:S(2)}, u32[]{:S(2)}) collective-permute-start(f32[8,128]{1,0:T(8,128)S(1)} %add.9.refs_0_), channel_id=1, source_target_pairs={{0,6},{1,7},{2,4},{3,5},{4,2},{5,3},{6,0},{7,1},{8,14},{9,15},{10,... | collective-permute-start | bytes 12296 | tf_op jit(solution)/shard_map/ppermute | solution.py:360
  50.8 4.5 %collective-permute-start.14 = (f32[8,128]{1,0:T(8,128)S(1)}, f32[8,128]{1,0:T(8,128)S(1)}, u32[]{:S(2)}, u32[]{:S(2)}) collective-permute-start(f32[8,128]{1,0:T(8,128)S(1)} %add.9.refs_0_), channel_id=1, source_target_pairs={{0,4},{1,5},{2,6},{3,7},{4,0},{5,1},{6,2},{7,3},{8,12},{9,13},{10,... | collective-permute-start | bytes 12296 | tf_op jit(solution)/shard_map/ppermute | solution.py:360
  50.8 4.5 %collective-permute-start.13 = (f32[8,128]{1,0:T(8,128)S(1)}, f32[8,128]{1,0:T(8,128)S(1)}, u32[]{:S(2)}, u32[]{:S(2)}) collective-permute-start(f32[8,128]{1,0:T(8,128)S(1)} %add.9.refs_0_), channel_id=1, source_target_pairs={{0,2},{1,3},{2,0},{3,1},{4,6},{5,7},{6,4},{7,5},{8,10},{9,11},{10,... | collective-permute-start | bytes 12296 | tf_op jit(solution)/shard_map/ppermute | solution.py:360

commit v4 on v3

--- a/solution.py
+++ b/solution.py
@@ -281,6 +281,12 @@
     go[...] = total[stay.shape[0] :, :].astype(jnp.bfloat16)
 
 
+def pad_kernel(cotangent, padded):
+    length = cotangent.shape[0]
+    padded[:length, :] = cotangent[...]
+    padded[length:, :] = jnp.zeros((padded.shape[0] - length, padded.shape[1]), padded.dtype)
+
+
 def far_kernel(n_seq, place, *refs):
     blocks, refs = refs[: 3 * n_seq], refs[3 * n_seq :]
     wq, wk, wv, table, xq, xkv, gq, gkv, grad, qw, kw, vw = refs
@@ -293,7 +299,7 @@
             rows = pl.ds(pl.multiple_of(s * length + side * half, half), half)
             xq[rows, :] = source[:, :QL]
             xkv[rows, :] = source[:, QL:LATENT]
-        grad[s * length : (s + 1) * length, :] = cotangent[...]
+        grad[s * length : (s + 1) * length, :] = cotangent[:length, :]
     ready = (lambda: None, lambda: None)
     backward(length, xq, xkv, grad, (wq, wk, wv), table, gq, gkv, qw, kw, vw, None, ready)
 
@@ -498,7 +504,18 @@
         if k not in received:
             relayed[k] = across(relayed[k & (k - 1)], n_dp, n_head, k & -k)
             received[k] = relayed[k]
-            cotangents[k] = across(cotangents[k & (k - 1)], n_dp, n_head, k & -k)
+            source = cotangents[k & (k - 1)]
+            if k & (k - 1) in singles:
+                source = pl.pallas_call(
+                    pad_kernel,
+                    out_shape=pltpu.VMEM((length + 32, wide_k), jnp.bfloat16),
+                    in_specs=vmem(1),
+                    out_specs=pl.BlockSpec(memory_space=pltpu.VMEM),
+                    compiler_params=params(),
+                    cost_estimate=free(),
+                    name="pad",
+                )(source)
+            cotangents[k] = across(source, n_dp, n_head, k & -k)
 
     def swapped(k):
         return exchange(received[turned_round(k, n_dp)], "head", n_head, 1)

time: 57.7 us -> 59.5 us (1.031)
  waiting for transfers between devices: 13.7 us -> 15.6 us
    ppermute x10, waiting for transfers between devices: 4.61 us -> 7.19 us  [exchange(): return lax.ppermute(value, axis, [(i, i ^ k) for i in range(size)])]
    ppermute x6, starting transfers between devices: 8.19 us -> 7.29 us  [across(): return lax.ppermute(value, ('dp', 'head'), pairs)]
    ppermute x10, starting transfers between devices: 10 us -> 10.9 us  [exchange(): return lax.ppermute(value, axis, [(i, i ^ k) for i in range(size)])]
    ppermute x6, waiting for transfers between devices: 9.11 us -> 8.45 us  [across(): return lax.ppermute(value, ('dp', 'head'), pairs)]
  transfers between devices with their start and end apart: 16 -> 16, of which waited for: 7 -> 7; matrix products, arithmetic and copies ran while one was open for 0% -> 0% of each run, Pallas kernels for 36% -> 35%
where the time goes in v4:
time: 59.5 us; the launch traced here: 59.4 us
  Pallas kernels  24.6 us (41%)
  starting transfers between devices  18.1 us (30%)
  waiting for transfers between devices  15.6 us (26%)
  between operations  0.93 us (2%)
    ppermute x10, starting transfers between devices, exchange(): return lax.ppermute(value, axis, [(i, i ^ k) for i in range(size)])  10.9 us
    ppermute x6, waiting for transfers between devices, across(): return lax.ppermute(value, ('dp', 'head'), pairs)  8.45 us
    pallas_call x2, Pallas kernels, per_device(): pl.pallas_call(functools.partial(far_kernel, n_seq), out_shape=rows_shape...  8.44 us
    ppermute x6, starting transfers between devices, across(): return lax.ppermute(value, ('dp', 'head'), pairs)  7.29 us
    ppermute x10, waiting for transfers between devices, exchange(): return lax.ppermute(value, axis, [(i, i ^ k) for i in range(size)])  7.19 us
    pallas_call x1, Pallas kernels, per_device(): pl.pallas_call(functools.partial(own_kernel, n_head), out_shape=(*weights...  6.09 us
    pallas_call x4, Pallas kernels, add_sums(): pl.pallas_call(functools.partial(sums_kernel, len(shapes), not sums), out...  4.02 us
    pallas_call x1, Pallas kernels, per_device(): pl.pallas_call(functools.partial(scale_kernel, limit), out_shape=(*[struc...  2.09 us
  transfers between devices with their start and end apart: 16, of which 7 were waited for; matrix products, arithmetic and copies ran while one was open for 0% of the time, Pallas kernels for 35%

profile of v4, /device:TPU:0, one launch (start us, length us, event | category | flops | bytes accessed | tf_op | source)
XLA Modules:
  0.0 59.4 jit_solution(5345622049394306906)
XLA Ops:
  0.7 1.7 %load.1 = (bf16[128,2176]{1,0:T(8,128)(2,1)S(1)}, bf16[256,512]{1,0:T(8,128)(2,1)S(1)}) custom-call(s32[2]{0:T(128)S(1)} %pad_add_fusion.place, bf16[256,1536]{1,0:T(8,128)(2,1)} %xq_in.1, bf16[576,256]{1,0:T(8,128)(2,1)} %bitcast.3, bf16[256,512]{1,0:T(8,128)(2,1)} %grad_in.1), custom_call_target="tpu_custom_call" | custom-call | tf_op jit(solution)/shard_map/load/pallas_call | solution.py:398
  2.4 3.0 %collective-permute-start.2 = (bf16[128,2176]{1,0:T(8,128)(2,1)S(1)}, bf16[128,2176]{1,0:T(8,128)(2,1)S(1)}, u32[]{:S(2)}, u32[]{:S(2)}) collective-permute-start(bf16[128,2176]{1,0:T(8,128)(2,1)S(1)} %get-tuple-element.68), channel_id=1, source_target_pairs={{0,16},{1,9},{2,18},{3,11},{4,20},{5,13},{6,22},{7,15},{8,24},{9,1... | collective-permute-start | bytes 1671176 | tf_op jit(solution)/shard_map/ppermute | solution.py:383
  5.5 1.5 %collective-permute-start.3 = (bf16[128,2176]{1,0:T(8,128)(2,1)S(1)}, bf16[128,2176]{1,0:T(8,128)(2,1)S(1)}, u32[]{:S(2)}, u32[]{:S(2)}) collective-permute-start(bf16[128,2176]{1,0:T(8,128)(2,1)S(1)} %get-tuple-element.68), channel_id=1, source_target_pairs={{0,8},{1,17},{2,10},{3,19},{4,12},{5,21},{6,14},{7,23},{8,0},{9,25... | collective-permute-start | bytes 1671176 | tf_op jit(solution)/shard_map/ppermute | solution.py:383
  7.0 6.1 %own.1 = (bf16[1536,768]{1,0:T(8,128)(2,1)S(1)}, bf16[512,512]{1,0:T(8,128)(2,1)S(1)}, bf16[512,512]{1,0:T(8,128)(2,1)S(1)}, f32[256,256]{1,0:T(8,128)S(1)}, bf1...) custom-call(s32[2]{0:T(128)S(1)} %pad_add_fusion.place, ...), custom_call_target="tpu_custom_call" | custom-call | tf_op jit(solution)/shard_map/own/pallas_call | solution.py:428
  14.3 0.8 %sums.4.refs_0_ = f32[1536,768]{1,0:T(8,128)S(1)} custom-call(bf16[256,1536]{1,0:T(8,128)(2,1)S(1)} %get-tuple-element.69.left, bf16[256,768]{1,0:T(8,128)(2,1)S(1)} %get-tuple-element.70.right), custom_call_target="tpu_custom_call" | custom-call | tf_op jit(solution)/shard_map/sums/pallas_call | solution.py:453
  15.1 3.3 %collective-permute-done.2.refs_3_ = bf16[128,2176]{1,0:T(8,128)(2,1)S(1)} collective-permute-done((bf16[128,2176]{1,0:T(8,128)(2,1)S(1)}, bf16[128,2176]{1,0:T(8,128)(2,1)S(1)}, u32[]{:S(2)}, u32[]{:S(2)}) %collective-permute-start.2) | collective-permute-done | bytes 557088 | tf_op jit(solution)/shard_map/ppermute | solution.py:383
  18.4 1.6 %collective-permute-done.3.refs_0_ = bf16[128,2176]{1,0:T(8,128)(2,1)S(1)} collective-permute-done((bf16[128,2176]{1,0:T(8,128)(2,1)S(1)}, bf16[128,2176]{1,0:T(8,128)(2,1)S(1)}, u32[]{:S(2)}, u32[]{:S(2)}) %collective-permute-start.3) | collective-permute-done | bytes 557088 | tf_op jit(solution)/shard_map/ppermute | solution.py:383
  20.6 3.5 %collective-permute-done.5.refs_5_.cotangent = bf16[256,512]{1,0:T(8,128)(2,1)S(1)} collective-permute-done((bf16[256,512]{1,0:T(8,128)(2,1)S(1)}, bf16[256,512]{1,0:T(8,128)(2,1)S(1)}, u32[]{:S(2)}, u32[]{:S(2)}) %collective-permute-start.5) | collective-permute-done | bytes 262176 | tf_op jit(solution)/shard_map/ppermute | solution.py:383
  24.1 1.5 %collective-permute-start.8 = (bf16[128,2176]{1,0:T(8,128)(2,1)S(1)}, bf16[128,2176]{1,0:T(8,128)(2,1)S(1)}, u32[]{:S(2)}, u32[]{:S(2)}) collective-permute-start(bf16[128,2176]{1,0:T(8,128)(2,1)S(1)} %collective-permute-done.2.refs_3_), channel_id=1, source_target_pairs={{0,8},{1,17},{2,10},{3,19},{4,12},{5,21},{6,14},{7,23},{8,0},{9,25... | collective-permute-start | bytes 1671176 | tf_op jit(solution)/shard_map/ppermute | solution.py:383
  25.5 0.6 %collective-permute-start.9 = (bf16[288,512]{1,0:T(8,128)(2,1)S(1)}, bf16[288,512]{1,0:T(8,128)(2,1)S(1)}, u32[]{:S(2)}, u32[]{:S(2)}) collective-permute-start(bf16[288,512]{1,0:T(8,128)(2,1)S(1)} %pad.5), channel_id=1, source_target_pairs={{0,8},{1,17},{2,10},{3,19},{4,12},{5,21},{6,14},{7,23},{8,0},{9,25... | collective-permute-start | bytes 884744 | tf_op jit(solution)/shard_map/ppermute | solution.py:383
  26.3 2.6 %collective-permute-start.1 = (bf16[64,2176]{1,0:T(8,128)(2,1)S(1)}, bf16[64,2176]{1,0:T(8,128)(2,1)S(1)}, u32[]{:S(2)}, u32[]{:S(2)}) collective-permute-start(bf16[64,2176]{1,0:T(8,128)(2,1)S(1)} %get-tuple-element.67), channel_id=1, source_target_pairs={{0,2},{1,3},{2,0},{3,1},{4,6},{5,7},{6,4},{7,5},{8,10},{9,11},{10,... | collective-permute-start | bytes 835592 | tf_op jit(solution)/shard_map/ppermute | solution.py:366
  28.9 5.2 %far.2 = (bf16[512,1536]{1,0:T(8,128)(2,1)S(1)}, bf16[512,576]{1,0:T(8,128)(2,1)S(1)}, bf16[512,768]{1,0:T(8,128)(2,1)S(1)}, bf16[512,1024]{1,0:T(8,128)(2,1)S(1)}) custom-call(s32[2]{0:T(128)S(1)} %pad_add_fusion.place, bf16[128,2176]{1,0:T(8,128)(2,1)S(1)} %collective-permute-done.3.refs_0_, bf16[128,2176]{1,0:T(8,128)(2,1)S(1)} %collective-permute-done.4.refs_1_, ...), custom_call_target="tpu_custom_call" | custom-call | tf_op jit(solution)/shard_map/far/pallas_call | solution.py:532
  34.2 1.1 %collective-permute-done.1.received = bf16[64,2176]{1,0:T(8,128)(2,1)S(1)} collective-permute-done((bf16[64,2176]{1,0:T(8,128)(2,1)S(1)}, bf16[64,2176]{1,0:T(8,128)(2,1)S(1)}, u32[]{:S(2)}, u32[]{:S(2)}) %collective-permute-start.1) | collective-permute-done | bytes 278560 | tf_op jit(solution)/shard_map/ppermute | solution.py:366
  35.3 1.9 %sums.6.pq = f32[1536,768]{1,0:T(8,128)S(1)} custom-call(bf16[512,1536]{1,0:T(8,128)(2,1)S(1)} %get-tuple-element.87.left, bf16[512,768]{1,0:T(8,128)(2,1)S(1)} %get-tuple-element.90.right, f32[1536,768]{1,0:T(8,128)S(1)} %sums.4.refs_0_), custom_call_target="tpu_custom_call", output_to_operand_aliasing={{}: (2, {})} | custom-call | tf_op jit(solution)/shard_map/sums/pallas_call | solution.py:453
  37.4 2.9 %collective-permute-start.12 = (bf16[32,2176]{1,0:T(8,128)(2,1)S(1)}, bf16[32,2176]{1,0:T(8,128)(2,1)S(1)}, u32[]{:S(2)}, u32[]{:S(2)}) collective-permute-start(bf16[32,2176]{1,0:T(8,128)(2,1)S(1)} %get-tuple-element.108), channel_id=1, source_target_pairs={{0,4},{1,5},{2,6},{3,7},{4,0},{5,1},{6,2},{7,3},{8,12},{9,13},{10,... | collective-permute-start | bytes 417800 | tf_op jit(solution)/shard_map/ppermute | solution.py:366
  40.3 0.8 %sums.7 = (f32[512,512]{1,0:T(8,128)S(1)}, f32[512,512]{1,0:T(8,128)S(1)}) custom-call(bf16[512,576]{1,0:T(8,128)(2,1)S(1)} %get-tuple-element.93.left, bf16[512,1024]{1,0:T(8,128)(2,1)S(1)} %get-tuple-element.94.right, f32[512,512]{1,0:T(8,128)S(1)} %get-tuple-element.95.refs_0_, ...), custom_call_target="tpu_custom_call", output_to_operand_aliasing={{0}: (2, {}), {1}: (3, {})} | custom-call | tf_op jit(solution)/shard_map/sums/pallas_call | solution.py:453
  41.1 3.2 %far.3 = (bf16[256,1536]{1,0:T(8,128)(2,1)S(1)}, bf16[256,576]{1,0:T(8,128)(2,1)S(1)}, bf16[256,768]{1,0:T(8,128)(2,1)S(1)}, bf16[256,1024]{1,0:T(8,128)(2,1)S(1)}) custom-call(s32[2]{0:T(128)S(1)} %pad_add_fusion.place, bf16[128,2176]{1,0:T(8,128)(2,1)S(1)} %collective-permute-done.8.refs_0_, bf16[128,2176]{1,0:T(8,128)(2,1)S(1)} %collective-permute-done.10.refs_1_, ...), custom_call_target="tpu_custom_call" | custom-call | tf_op jit(solution)/shard_map/far/pallas_call | solution.py:532
  44.3 2.0 %last.1 = (f32[1536,768]{1,0:T(8,128)S(1)}, f32[512,512]{1,0:T(8,128)S(1)}, f32[512,512]{1,0:T(8,128)S(1)}, f32[8,128]{1,0:T(8,128)S(1)}) custom-call(bf16[256,1536]{1,0:T(8,128)(2,1)S(1)} %get-tuple-element.100.xq, bf16[256,576]{1,0:T(8,128)(2,1)S(1)} %get-tuple-element.101.xkv, ...), custom_call_target="tpu_custom_call", output_to_operand_aliasing={{0}: (4, {}), {1}: (5, {}), {2}: (6, {})} | custom-call | tf_op jit(solution)/shard_map/last/pallas_call | solution.py:557
  46.7 0.9 %collective-permute-done.11.right = f32[8,128]{1,0:T(8,128)S(1)} collective-permute-done((f32[8,128]{1,0:T(8,128)S(1)}, f32[8,128]{1,0:T(8,128)S(1)}, u32[]{:S(2)}, u32[]{:S(2)}) %collective-permute-start.11) | collective-permute-done | bytes 4128 | tf_op jit(solution)/shard_map/ppermute | solution.py:366
  47.6 1.6 %collective-permute-start.13 = (f32[8,128]{1,0:T(8,128)S(1)}, f32[8,128]{1,0:T(8,128)S(1)}, u32[]{:S(2)}, u32[]{:S(2)}) collective-permute-start(f32[8,128]{1,0:T(8,128)S(1)} %add.9.refs_0_), channel_id=1, source_target_pairs={{0,2},{1,3},{2,0},{3,1},{4,6},{5,7},{6,4},{7,5},{8,10},{9,11},{10,... | collective-permute-start | bytes 12296 | tf_op jit(solution)/shard_map/ppermute | solution.py:366
  49.2 2.5 %collective-permute-start.14 = (f32[8,128]{1,0:T(8,128)S(1)}, f32[8,128]{1,0:T(8,128)S(1)}, u32[]{:S(2)}, u32[]{:S(2)}) collective-permute-start(f32[8,128]{1,0:T(8,128)S(1)} %add.9.refs_0_), channel_id=1, source_target_pairs={{0,4},{1,5},{2,6},{3,7},{4,0},{5,1},{6,2},{7,3},{8,12},{9,13},{10,... | collective-permute-start | bytes 12296 | tf_op jit(solution)/shard_map/ppermute | solution.py:366
  52.0 1.7 %collective-permute-done.14.refs_2_ = f32[8,128]{1,0:T(8,128)S(1)} collective-permute-done((f32[8,128]{1,0:T(8,128)S(1)}, f32[8,128]{1,0:T(8,128)S(1)}, u32[]{:S(2)}, u32[]{:S(2)}) %collective-permute-start.14) | collective-permute-done | bytes 4128 | tf_op jit(solution)/shard_map/ppermute | solution.py:366
  53.7 3.4 %collective-permute-done.15.refs_3_ = f32[8,128]{1,0:T(8,128)S(1)} collective-permute-done((f32[8,128]{1,0:T(8,128)S(1)}, f32[8,128]{1,0:T(8,128)S(1)}, u32[]{:S(2)}, u32[]{:S(2)}) %collective-permute-start.15) | collective-permute-done | bytes 4128 | tf_op jit(solution)/shard_map/ppermute | solution.py:366
  57.1 2.1 %scale.1 = (bf16[1536,768]{1,0:T(8,128)(2,1)}, bf16[512,512]{1,0:T(8,128)(2,1)}, bf16[512,512]{1,0:T(8,128)(2,1)}, f32[32,1536]{1,0:T(8,128)}, f32[32,576]{1,0:T(8,128)}) custom-call(f32[32,2176]{1,0:T(8,128)S(1)} %get-tuple-element.85.local, bf16[32,2176]{1,0:T(8,128)(2,1)S(1)} %collective-permute-done.12.received, f32[1536,768]{1,0:T(8,128)S(1)} %get-tuple-element.110.sq, ...), custom_call_target="tpu_custom_call" | custom-call | tf_op jit(solution)/shard_map/scale/pallas_call | solution.py:573
  (23 shorter events, 2.7 us)
Async XLA Ops:
  2.4 16.0 %collective-permute-start.2 = (bf16[128,2176]{1,0:T(8,128)(2,1)S(1)}, bf16[128,2176]{1,0:T(8,128)(2,1)S(1)}, u32[]{:S(2)}, u32[]{:S(2)}) collective-permute-start(bf16[128,2176]{1,0:T(8,128)(2,1)S(1)} %get-tuple-element.68), channel_id=1, source_target_pairs={{0,16},{1,9},{2,18},{3,11},{4,20},{5,13},{6,22},{7,15},{8,24},{9,1... | collective-permute-start | bytes 1671176 | tf_op jit(solution)/shard_map/ppermute | solution.py:383
  5.5 14.6 %collective-permute-start.3 = (bf16[128,2176]{1,0:T(8,128)(2,1)S(1)}, bf16[128,2176]{1,0:T(8,128)(2,1)S(1)}, u32[]{:S(2)}, u32[]{:S(2)}) collective-permute-start(bf16[128,2176]{1,0:T(8,128)(2,1)S(1)} %get-tuple-element.68), channel_id=1, source_target_pairs={{0,8},{1,17},{2,10},{3,19},{4,12},{5,21},{6,14},{7,23},{8,0},{9,25... | collective-permute-start | bytes 1671176 | tf_op jit(solution)/shard_map/ppermute | solution.py:383
  13.1 13.1 %collective-permute-start = (bf16[128,2176]{1,0:T(8,128)(2,1)S(1)}, bf16[128,2176]{1,0:T(8,128)(2,1)S(1)}, u32[]{:S(2)}, u32[]{:S(2)}) collective-permute-start(bf16[128,2176]{1,0:T(8,128)(2,1)S(1)} %get-tuple-element.65), channel_id=1, source_target_pairs={{0,1},{1,0},{2,3},{3,2},{4,5},{5,4},{6,7},{7,6},{8,9},{9,8},{10,11... | collective-permute-start | bytes 1671176 | tf_op jit(solution)/shard_map/ppermute | solution.py:366
  13.1 10.9 %collective-permute-start.5 = (bf16[256,512]{1,0:T(8,128)(2,1)S(1)}, bf16[256,512]{1,0:T(8,128)(2,1)S(1)}, u32[]{:S(2)}, u32[]{:S(2)}) collective-permute-start(bf16[256,512]{1,0:T(8,128)(2,1)S(1)} %get-tuple-element.76), channel_id=1, source_target_pairs={{0,16},{1,9},{2,18},{3,11},{4,20},{5,13},{6,22},{7,15},{8,24},{9,1... | collective-permute-start | bytes 786440 | tf_op jit(solution)/shard_map/ppermute | solution.py:383
  13.7 10.3 %collective-permute-start.6 = (bf16[256,512]{1,0:T(8,128)(2,1)S(1)}, bf16[256,512]{1,0:T(8,128)(2,1)S(1)}, u32[]{:S(2)}, u32[]{:S(2)}) collective-permute-start(bf16[256,512]{1,0:T(8,128)(2,1)S(1)} %get-tuple-element.76), channel_id=1, source_target_pairs={{0,8},{1,17},{2,10},{3,19},{4,12},{5,21},{6,14},{7,23},{8,0},{9,25... | collective-permute-start | bytes 786440 | tf_op jit(solution)/shard_map/ppermute | solution.py:383
  20.1 8.8 %collective-permute-start.4 = (bf16[128,2176]{1,0:T(8,128)(2,1)S(1)}, bf16[128,2176]{1,0:T(8,128)(2,1)S(1)}, u32[]{:S(2)}, u32[]{:S(2)}) collective-permute-start(bf16[128,2176]{1,0:T(8,128)(2,1)S(1)} %collective-permute-done.2.refs_3_), channel_id=1, source_target_pairs={{0,1},{1,0},{2,3},{3,2},{4,5},{5,4},{6,7},{7,6},{8,9},{9,8},{10,11... | collective-permute-start | bytes 1671176 | tf_op jit(solution)/shard_map/ppermute | solution.py:366
  20.1 8.8 %collective-permute-start.7 = (bf16[128,2176]{1,0:T(8,128)(2,1)S(1)}, bf16[128,2176]{1,0:T(8,128)(2,1)S(1)}, u32[]{:S(2)}, u32[]{:S(2)}) collective-permute-start(bf16[128,2176]{1,0:T(8,128)(2,1)S(1)} %collective-permute-done.3.refs_0_), channel_id=1, source_target_pairs={{0,1},{1,0},{2,3},{3,2},{4,5},{5,4},{6,7},{7,6},{8,9},{9,8},{10,11... | collective-permute-start | bytes 1671176 | tf_op jit(solution)/shard_map/ppermute | solution.py:366
  24.1 13.2 %collective-permute-start.8 = (bf16[128,2176]{1,0:T(8,128)(2,1)S(1)}, bf16[128,2176]{1,0:T(8,128)(2,1)S(1)}, u32[]{:S(2)}, u32[]{:S(2)}) collective-permute-start(bf16[128,2176]{1,0:T(8,128)(2,1)S(1)} %collective-permute-done.2.refs_3_), channel_id=1, source_target_pairs={{0,8},{1,17},{2,10},{3,19},{4,12},{5,21},{6,14},{7,23},{8,0},{9,25... | collective-permute-start | bytes 1671176 | tf_op jit(solution)/shard_map/ppermute | solution.py:383
  25.5 11.7 %collective-permute-start.9 = (bf16[288,512]{1,0:T(8,128)(2,1)S(1)}, bf16[288,512]{1,0:T(8,128)(2,1)S(1)}, u32[]{:S(2)}, u32[]{:S(2)}) collective-permute-start(bf16[288,512]{1,0:T(8,128)(2,1)S(1)} %pad.5), channel_id=1, source_target_pairs={{0,8},{1,17},{2,10},{3,19},{4,12},{5,21},{6,14},{7,23},{8,0},{9,25... | collective-permute-start | bytes 884744 | tf_op jit(solution)/shard_map/ppermute | solution.py:383
  26.3 9.0 %collective-permute-start.1 = (bf16[64,2176]{1,0:T(8,128)(2,1)S(1)}, bf16[64,2176]{1,0:T(8,128)(2,1)S(1)}, u32[]{:S(2)}, u32[]{:S(2)}) collective-permute-start(bf16[64,2176]{1,0:T(8,128)(2,1)S(1)} %get-tuple-element.67), channel_id=1, source_target_pairs={{0,2},{1,3},{2,0},{3,1},{4,6},{5,7},{6,4},{7,5},{8,10},{9,11},{10,... | collective-permute-start | bytes 835592 | tf_op jit(solution)/shard_map/ppermute | solution.py:366
  37.3 3.8 %collective-permute-start.10 = (bf16[128,2176]{1,0:T(8,128)(2,1)S(1)}, bf16[128,2176]{1,0:T(8,128)(2,1)S(1)}, u32[]{:S(2)}, u32[]{:S(2)}) collective-permute-start(bf16[128,2176]{1,0:T(8,128)(2,1)S(1)} %collective-permute-done.8.refs_0_), channel_id=1, source_target_pairs={{0,1},{1,0},{2,3},{3,2},{4,5},{5,4},{6,7},{7,6},{8,9},{9,8},{10,11... | collective-permute-start | bytes 1671176 | tf_op jit(solution)/shard_map/ppermute | solution.py:366
  37.4 10.2 %collective-permute-start.12 = (bf16[32,2176]{1,0:T(8,128)(2,1)S(1)}, bf16[32,2176]{1,0:T(8,128)(2,1)S(1)}, u32[]{:S(2)}, u32[]{:S(2)}) collective-permute-start(bf16[32,2176]{1,0:T(8,128)(2,1)S(1)} %get-tuple-element.108), channel_id=1, source_target_pairs={{0,4},{1,5},{2,6},{3,7},{4,0},{5,1},{6,2},{7,3},{8,12},{9,13},{10,... | collective-permute-start | bytes 417800 | tf_op jit(solution)/shard_map/ppermute | solution.py:366
  46.4 1.2 %collective-permute-start.11 = (f32[8,128]{1,0:T(8,128)S(1)}, f32[8,128]{1,0:T(8,128)S(1)}, u32[]{:S(2)}, u32[]{:S(2)}) collective-permute-start(f32[8,128]{1,0:T(8,128)S(1)} %get-tuple-element.107.left), channel_id=1, source_target_pairs={{0,1},{1,0},{2,3},{3,2},{4,5},{5,4},{6,7},{7,6},{8,9},{9,8},{10,11... | collective-permute-start | bytes 12296 | tf_op jit(solution)/shard_map/ppermute | solution.py:366
  47.6 4.4 %collective-permute-start.13 = (f32[8,128]{1,0:T(8,128)S(1)}, f32[8,128]{1,0:T(8,128)S(1)}, u32[]{:S(2)}, u32[]{:S(2)}) collective-permute-start(f32[8,128]{1,0:T(8,128)S(1)} %add.9.refs_0_), channel_id=1, source_target_pairs={{0,2},{1,3},{2,0},{3,1},{4,6},{5,7},{6,4},{7,5},{8,10},{9,11},{10,... | collective-permute-start | bytes 12296 | tf_op jit(solution)/shard_map/ppermute | solution.py:366
  49.2 4.5 %collective-permute-start.14 = (f32[8,128]{1,0:T(8,128)S(1)}, f32[8,128]{1,0:T(8,128)S(1)}, u32[]{:S(2)}, u32[]{:S(2)}) collective-permute-start(f32[8,128]{1,0:T(8,128)S(1)} %add.9.refs_0_), channel_id=1, source_target_pairs={{0,4},{1,5},{2,6},{3,7},{4,0},{5,1},{6,2},{7,3},{8,12},{9,13},{10,... | collective-permute-start | bytes 12296 | tf_op jit(solution)/shard_map/ppermute | solution.py:366
  51.7 5.4 %collective-permute-start.15 = (f32[8,128]{1,0:T(8,128)S(1)}, f32[8,128]{1,0:T(8,128)S(1)}, u32[]{:S(2)}, u32[]{:S(2)}) collective-permute-start(f32[8,128]{1,0:T(8,128)S(1)} %add.9.refs_0_), channel_id=1, source_target_pairs={{0,6},{1,7},{2,4},{3,5},{4,2},{5,3},{6,0},{7,1},{8,14},{9,15},{10,... | collective-permute-start | bytes 12296 | tf_op jit(solution)/shard_map/ppermute | solution.py:366
